TPU v7x, 256 devices: a whole 4x4x8 slice. The times are simulated.
256 devices in a mesh: inst: 16 (over x_lo, z), mesh: 16 (over x_hi, y, core).
Axes of the slice: x: 4 (x_hi: 2, x_lo: 2; x = x_hi * 2 + x_lo), y: 4, z: 8, core: 2. Of those that a mesh axis runs over, the one named last changes fastest.
Arguments:
- tangent_in: bfloat16 [16, 4, 64, 2048], P('inst', None, None, 'mesh'), may hold values from -6 to 6
- adjoint_in: bfloat16 [16, 4, 64, 2048], P('inst', None, None, 'mesh'), may hold values from -6 to 6
- jacobian: bfloat16 [16, 5, 64, 64, 2048], P('inst', None, None, None, 'mesh'), may hold values from -0.3125 to 0.3125
- neighbors: int32 [2, 4, 2048], P(None, None, 'mesh'), may hold values from 0 to 192, as said below
- send_low: int32 [2, 512], P(None, 'mesh'), may hold values from 0 to 127, as said below
- send_high: int32 [2, 512], P(None, 'mesh'), may hold values from 0 to 127, as said below
- frequency: float32 [1], replicated, may hold values from 0.05 to 0.2
Outputs:
- tangent_out: bfloat16 [16, 4, 64, 2048], P('inst', None, None, 'mesh')
- adjoint_out: bfloat16 [16, 4, 64, 2048], P('inst', None, None, 'mesh')
Inputs may be any that keep to these rules, and one draw needn't show every extreme that they name: `neighbors`: extended row indices: below 128 a row of the slab itself, 128 to 159 rows received from the slab below, the next 32 rows received from the slab above, 192 the zero row. `send_low`: each slab's 32 entries are distinct block rows of that slab. `send_high`: each slab's 32 entries are distinct block rows of that slab.
All inputs are finite; a program needn't handle non-finite values.
Results may differ from a plain program's by a relative error of at most 0.003.
Values may be sent and summed in bfloat16 or wider, within the bound.
No kernel may reach another device: no remote copies, remote signals or barrier semaphores. Data moves between devices by JAX's collectives and lax.ppermute only.
A program may use at most 64 MiB of HBM per device.

v0:
```python
import math

import jax
import jax.numpy as jnp
from jax import lax
from jax.sharding import PartitionSpec as P

INST = 8


def passed_along(value, axis, steps):
    count = lax.axis_size(axis)
    leading, last = (max(0, -steps), min(count, count - steps))
    return lax.ppermute(value, axis, [(source, source + steps) for source in range(leading, last)])


def from_behind(block, axis, distance):
    devices = range(lax.axis_size(axis))
    route = [((i - distance) % len(devices), i) for i in devices]
    return lax.ppermute(block, axis, route)


def coefficient(distance, frequency):
    parity = 1.0 - 2.0 * (distance % 2)
    value = parity * math.cos(math.pi * distance / INST) / math.sin(math.pi * distance / INST)
    return frequency[0] * (0.5 * value)


def body(tangent_in, adjoint_in, jacobian, neighbors, send_low, send_high, frequency):
    groups = tangent_in.shape[0]
    columns = tangent_in.shape[1]
    block = tangent_in.shape[2]
    local_rows = tangent_in.shape[3]
    halo_rows = send_low.shape[1]
    sides = lax.axis_size("inst") // INST
    side = lax.axis_index("inst") % sides
    slab = side * lax.axis_size("mesh") + lax.axis_index("mesh")
    last_slab = sides * lax.axis_size("mesh") - 1
    width = local_rows + 2 * halo_rows + 1
    near = lax.dynamic_index_in_dim(neighbors, side, 0, keepdims=False)
    low_idx = lax.dynamic_index_in_dim(send_low, side, 0, keepdims=False)
    high_idx = lax.dynamic_index_in_dim(send_high, side, 0, keepdims=False)
    contrib = jnp.einsum(
        "ikabn,ican->icbkn", jacobian, adjoint_in, preferred_element_type=jnp.float32
    )
    spread_terms = contrib[:, :, :, 1:, :].reshape(groups, columns, block, -1)
    spread = (
        jnp.zeros((groups, columns, block, width), jnp.float32)
        .at[..., near.reshape(-1)]
        .add(spread_terms)
    )
    own = spread[..., :local_rows] + contrib[:, :, :, 0, :]
    back_down = spread[..., local_rows : local_rows + halo_rows].astype(jnp.bfloat16)
    back_up = spread[..., local_rows + halo_rows : local_rows + 2 * halo_rows].astype(jnp.bfloat16)
    rows_high = jnp.take(tangent_in, high_idx, axis=3)
    rows_low = jnp.take(tangent_in, low_idx, axis=3)
    below_rows, from_below = passed_along((rows_high, back_up), ("inst", "mesh"), 1)
    above_rows, from_above = passed_along((rows_low, back_down), ("inst", "mesh"), -1)
    has_below = slab > 0
    has_above = slab < last_slab
    below_rows = jnp.where(has_below, below_rows, jnp.zeros_like(below_rows))
    from_below = jnp.where(has_below, from_below, jnp.zeros_like(from_below))
    above_rows = jnp.where(has_above, above_rows, jnp.zeros_like(above_rows))
    from_above = jnp.where(has_above, from_above, jnp.zeros_like(from_above))
    own = own.at[..., low_idx].add(from_below.astype(jnp.float32))
    own = own.at[..., high_idx].add(from_above.astype(jnp.float32))
    blank = jnp.zeros((groups, columns, block, 1), tangent_in.dtype)
    extended = jnp.concatenate([tangent_in, below_rows, above_rows, blank], axis=3)
    picked = jnp.take(extended, near, axis=3)
    stacked = jnp.concatenate([tangent_in[:, :, :, None, :], picked], axis=3)
    image = jnp.einsum("ikabn,icbkn->ican", jacobian, stacked, preferred_element_type=jnp.float32)
    tangent_spec = jnp.zeros((groups, columns, block, local_rows), jnp.float32)
    adjoint_spec = jnp.zeros((groups, columns, block, local_rows), jnp.float32)
    carried = (tangent_in, adjoint_in)
    for distance in range(1, INST):
        carried = from_behind((carried[0], carried[1]), "inst", sides)
        factor = coefficient(distance, frequency)
        tangent_spec = tangent_spec + factor * carried[0].astype(jnp.float32)
        adjoint_spec = adjoint_spec - factor * carried[1].astype(jnp.float32)
    tangent_out = (image + tangent_spec).astype(jnp.bfloat16)
    adjoint_out = (own + adjoint_spec).astype(jnp.bfloat16)
    return (tangent_out, adjoint_out)


def solution(mesh):
    in_specs = (
        P("inst", None, None, "mesh"),
        P("inst", None, None, "mesh"),
        P("inst", None, None, None, "mesh"),
        P(None, None, "mesh"),
        P(None, "mesh"),
        P(None, "mesh"),
        P(),
    )
    out_specs = (P("inst", None, None, "mesh"), P("inst", None, None, "mesh"))
    return jax.shard_map(body, mesh=mesh, in_specs=in_specs, out_specs=out_specs, check_vma=False)
```

profile of v0, /device:TPU:2, one launch (start us, length us, event | category | flops | bytes accessed | tf_op | source)
XLA Modules:
  0.0 129.8 jit_solution(16348555424761593343)
XLA Ops:
  0.7 3.3 %collective-permute-start.2 = (bf16[1,4,64,128]{3,2,1,0:T(8,128)(2,1)}, bf16[1,4,64,128]{3,2,1,0:T(8,128)(2,1)S(1)}, u32[]{:S(2)}, u32[]{:S(2)}) collective-permute-start(bf16[1,4,64,128]{3,2,1,0:T(8,128)(2,1)} %param.9), channel_id=1, source_target_pairs={{224,0},{240,16},{0,32},{16,48},{32,64},{48,80},{64,96},{80,112},{... | collective-permute-start | bytes 196616 | tf_op jit(solution)/shard_map/ppermute | solution.py:20
  4.0 1.0 copy.56
  5.0 0.7 compare_and_fusion
  5.7 0.6 gather_fusion.2
  6.5 0.6 bitcast_select_fusion.1
  7.1 7.3 %collective-permute-start.1 = (bf16[1,4,64,32]{3,2,1,0:T(8,128)(2,1)}, bf16[1,4,64,32]{3,2,1,0:T(8,128)(2,1)S(1)}, u32[]{:S(2)}, u32[]{:S(2)}) collective-permute-start(bf16[1,4,64,32]{3,2,1,0:T(8,128)(2,1)} %bitcast_select_fusion.1), channel_id=1, source_target_pairs={{1,0},{2,1},{3,2},{4,3},{5,4},{6,5},{7,6},{8,7},{9,8},{10,9},{11,1... | collective-permute-start | bytes 49160 | tf_op jit(solution)/shard_map/ppermute | solution.py:14
  14.4 0.6 gather_fusion.1
  15.2 1.9 %collective-permute-start = (bf16[1,4,64,32]{3,2,1,0:T(8,128)(2,1)S(1)}, bf16[1,4,64,32]{3,2,1,0:T(8,128)(2,1)S(1)}, u32[]{:S(2)}, u32[]{:S(2)}) collective-permute-start(bf16[1,4,64,32]{3,2,1,0:T(8,128)(2,1)S(1)} %bitcast_select_fusion.2), channel_id=1, source_target_pairs={{0,1},{1,2},{2,3},{3,4},{4,5},{5,6},{6,7},{7,8},{8,9},{9,10},{10,1... | collective-permute-start | bytes 49160 | tf_op jit(solution)/shard_map/ppermute | solution.py:14
  17.1 1.2 collective-permute-start.9
  18.3 15.8 %copy.67 = bf16[5,64,64,128]{2,1,0,3:T(8,128)(2,1)} copy(bf16[5,64,64,128]{3,2,1,0:T(8,128)(2,1)} %bitcast.97) | data formatting | bytes 10485760 | tf_op jit(solution)/shard_map/reshape.5
  34.1 0.1 copy.80
  34.3 5.7 %fusion.11 = f32[128,4,5,64]{3,1,2,0:T(4,128)S(1)} fusion(bf16[4,64,128,1]{1,0,3,2:T(4,128)(2,1)S(1)} %copy.80, bf16[5,64,64,128]{2,1,0,3:T(8,128)(2,1)} %copy.67), kind=kOutput, calls=%fused_computation.47 | convolution fusion | flops 20971520 | bytes 5963776 | tf_op jit(solution)/shard_map/ikabn,ican->icbkn/dot_general | solution.py:43
  40.0 1.0 copy.71
  41.1 0.3 copy.72
  41.4 0.2 reshape.212
  41.7 0.4 copy.73
  42.1 16.7 %scatter_fusion = f32[4,64,193]{1,0,2:T(4,128)S(1)} fusion(f32[4,64,193]{1,0,2:T(4,128)S(1)} %broadcast.114, s32[512]{0:T(512)S(1)} %bitcast.108, f32[512,4,64]{2,1,0:T(4,128)S(1)} %copy.73), kind=kCustom, calls=%fused_computation.3 | custom fusion | flops 131072 | bytes 1574912 | tf_op jit(solution)/shard_map/scatter-add | solution.py:50
  58.9 0.2 copy.74
  59.2 1.9 %collective-permute-start.16 = (bf16[1,4,64,32]{3,2,1,0:T(8,128)(2,1)S(1)}, bf16[1,4,64,32]{3,2,1,0:T(8,128)(2,1)S(1)}, u32[]{:S(2)}, u32[]{:S(2)}) collective-permute-start(bf16[1,4,64,32]{3,2,1,0:T(8,128)(2,1)S(1)} %get-tuple-element.18), channel_id=1, source_target_pairs={{0,1},{1,2},{2,3},{3,4},{4,5},{5,6},{6,7},{7,8},{8,9},{9,10},{10,1... | collective-permute-start | bytes 49160 | tf_op jit(solution)/shard_map/ppermute | solution.py:14
  61.2 0.1 copy.57
  62.1 9.1 %collective-permute-start.17 = (bf16[1,4,64,32]{3,2,1,0:T(8,128)(2,1)S(1)}, bf16[1,4,64,32]{3,2,1,0:T(8,128)(2,1)S(1)}, u32[]{:S(2)}, u32[]{:S(2)}) collective-permute-start(bf16[1,4,64,32]{3,2,1,0:T(8,128)(2,1)S(1)} %get-tuple-element.17), channel_id=1, source_target_pairs={{1,0},{2,1},{3,2},{4,3},{5,4},{6,5},{7,6},{8,7},{9,8},{10,9},{11,1... | collective-permute-start | bytes 49160 | tf_op jit(solution)/shard_map/ppermute | solution.py:14
  71.2 4.0 %collective-permute-start.10 = (bf16[1,4,64,128]{3,2,1,0:T(8,128)(2,1)S(1)}, bf16[1,4,64,128]{3,2,1,0:T(8,128)(2,1)S(1)}, u32[]{:S(2)}, u32[]{:S(2)}) collective-permute-start(bf16[1,4,64,128]{3,2,1,0:T(8,128)(2,1)S(1)} %collective-permute-done.9), channel_id=1, source_target_pairs={{224,0},{240,16},{0,32},{16,48},{32,64},{48,80},{64,96},{80,112},{... | collective-permute-start | bytes 196616 | tf_op jit(solution)/shard_map/ppermute | solution.py:20
  75.4 1.5 %collective-permute-start.3 = (bf16[1,4,64,128]{3,2,1,0:T(8,128)(2,1)S(1)}, bf16[1,4,64,128]{3,2,1,0:T(8,128)(2,1)S(1)}, u32[]{:S(2)}, u32[]{:S(2)}) collective-permute-start(bf16[1,4,64,128]{3,2,1,0:T(8,128)(2,1)S(1)} %collective-permute-done.2), channel_id=1, source_target_pairs={{224,0},{240,16},{0,32},{16,48},{32,64},{48,80},{64,96},{80,112},{... | collective-permute-start | bytes 196616 | tf_op jit(solution)/shard_map/ppermute | solution.py:20
  76.9 1.9 %collective-permute-done.10 = bf16[1,4,64,128]{3,2,1,0:T(8,128)(2,1)S(1)} collective-permute-done((bf16[1,4,64,128]{3,2,1,0:T(8,128)(2,1)S(1)}, bf16[1,4,64,128]{3,2,1,0:T(8,128)(2,1)S(1)}, u32[]{:S(2)}, u32[]{:S(2)}) %collective-permute-start.10) | collective-permute-done | bytes 65568 | tf_op jit(solution)/shard_map/ppermute | solution.py:20
  78.9 1.6 %collective-permute-start.11 = (bf16[1,4,64,128]{3,2,1,0:T(8,128)(2,1)S(1)}, bf16[1,4,64,128]{3,2,1,0:T(8,128)(2,1)S(1)}, u32[]{:S(2)}, u32[]{:S(2)}) collective-permute-start(bf16[1,4,64,128]{3,2,1,0:T(8,128)(2,1)S(1)} %collective-permute-done.10), channel_id=1, source_target_pairs={{224,0},{240,16},{0,32},{16,48},{32,64},{48,80},{64,96},{80,112},{... | collective-permute-start | bytes 196616 | tf_op jit(solution)/shard_map/ppermute | solution.py:20
  80.4 0.3 maximum_bitcast_fusion.2
  80.7 2.1 %gather_fusion = bf16[512,4,64]{2,1,0:T(4,128)(2,1)S(1)} fusion(bf16[4,64,193]{1,0,2:T(4,128)(2,1)S(1)} %maximum_bitcast_fusion.2, s32[1024]{0:T(1024)S(1)} %pad_clamp_fusion), kind=kCustom, calls=%fused_computation.2 | custom fusion | bytes 526336 | tf_op jit(solution)/shard_map/jit(_take)/gather | solution.py:69
  82.8 2.4 %collective-permute-done.3 = bf16[1,4,64,128]{3,2,1,0:T(8,128)(2,1)S(1)} collective-permute-done((bf16[1,4,64,128]{3,2,1,0:T(8,128)(2,1)S(1)}, bf16[1,4,64,128]{3,2,1,0:T(8,128)(2,1)S(1)}, u32[]{:S(2)}, u32[]{:S(2)}) %collective-permute-start.3) | collective-permute-done | bytes 65568 | tf_op jit(solution)/shard_map/ppermute | solution.py:20
  85.2 1.2 collective-permute-start.4
  86.4 1.0 collective-permute-done.11
  87.4 1.0 collective-permute-start.12
  88.4 0.8 bitcast_select_fusion
  89.2 5.9 %collective-permute-done.4 = bf16[1,4,64,128]{3,2,1,0:T(8,128)(2,1)S(1)} collective-permute-done((bf16[1,4,64,128]{3,2,1,0:T(8,128)(2,1)S(1)}, bf16[1,4,64,128]{3,2,1,0:T(8,128)(2,1)S(1)}, u32[]{:S(2)}, u32[]{:S(2)}) %collective-permute-start.4) | collective-permute-done | bytes 65568 | tf_op jit(solution)/shard_map/ppermute | solution.py:20
  95.2 0.8 collective-permute-done.12
  95.9 0.4 collective-permute-start.13
  96.3 7.3 %convolution_bitcast_fusion = f32[128,4,64]{2,1,0:T(4,128)S(1)} fusion(bf16[5,64,64,128]{2,1,0,3:T(8,128)(2,1)} %copy.67, bf16[1,4,64,4,128]{2,1,3,4,0:T(4,128)(2,1)S(1)} %bitcast_select_fusion, bf16[1,4,64,1,128]{2,1,3,4,0:T(4,128)(2,1)S(1)} %bitcast.102), kind=kOutput, calls=%fused_computation.6 | convolution fusion | flops 21626880 | bytes 5701632 | tf_op jit(solution)/shard_map/ikabn,icbkn->ican/dot_general | solution.py:71
  103.6 4.6 %collective-permute-start.6 = (bf16[1,4,64,128]{3,2,1,0:T(8,128)(2,1)S(1)}, bf16[1,4,64,128]{3,2,1,0:T(8,128)(2,1)S(1)}, u32[]{:S(2)}, u32[]{:S(2)}) collective-permute-start(bf16[1,4,64,128]{3,2,1,0:T(8,128)(2,1)S(1)} %collective-permute-done.5), channel_id=1, source_target_pairs={{224,0},{240,16},{0,32},{16,48},{32,64},{48,80},{64,96},{80,112},{... | collective-permute-start | bytes 196616 | tf_op jit(solution)/shard_map/ppermute | solution.py:20
  108.3 4.1 %collective-permute-done.6 = bf16[1,4,64,128]{3,2,1,0:T(8,128)(2,1)S(1)} collective-permute-done((bf16[1,4,64,128]{3,2,1,0:T(8,128)(2,1)S(1)}, bf16[1,4,64,128]{3,2,1,0:T(8,128)(2,1)S(1)}, u32[]{:S(2)}, u32[]{:S(2)}) %collective-permute-start.6) | collective-permute-done | bytes 65568 | tf_op jit(solution)/shard_map/ppermute | solution.py:20
  112.4 3.5 %collective-permute-start.7 = (bf16[1,4,64,128]{3,2,1,0:T(8,128)(2,1)S(1)}, bf16[1,4,64,128]{3,2,1,0:T(8,128)(2,1)S(1)}, u32[]{:S(2)}, u32[]{:S(2)}) collective-permute-start(bf16[1,4,64,128]{3,2,1,0:T(8,128)(2,1)S(1)} %collective-permute-done.6), channel_id=1, source_target_pairs={{224,0},{240,16},{0,32},{16,48},{32,64},{48,80},{64,96},{80,112},{... | collective-permute-start | bytes 196616 | tf_op jit(solution)/shard_map/ppermute | solution.py:20
  116.0 1.5 %collective-permute-done.14 = bf16[1,4,64,128]{3,2,1,0:T(8,128)(2,1)S(1)} collective-permute-done((bf16[1,4,64,128]{3,2,1,0:T(8,128)(2,1)S(1)}, bf16[1,4,64,128]{3,2,1,0:T(8,128)(2,1)S(1)}, u32[]{:S(2)}, u32[]{:S(2)}) %collective-permute-start.14) | collective-permute-done | bytes 65568 | tf_op jit(solution)/shard_map/ppermute | solution.py:20
  117.8 1.9 %collective-permute-done.7 = bf16[1,4,64,128]{3,2,1,0:T(8,128)(2,1)S(1)} collective-permute-done((bf16[1,4,64,128]{3,2,1,0:T(8,128)(2,1)S(1)}, bf16[1,4,64,128]{3,2,1,0:T(8,128)(2,1)S(1)}, u32[]{:S(2)}, u32[]{:S(2)}) %collective-permute-start.7) | collective-permute-done | bytes 65568 | tf_op jit(solution)/shard_map/ppermute | solution.py:20
  119.7 1.4 %collective-permute-start.8 = (bf16[1,4,64,128]{3,2,1,0:T(8,128)(2,1)S(1)}, bf16[1,4,64,128]{3,2,1,0:T(8,128)(2,1)S(1)}, u32[]{:S(2)}, u32[]{:S(2)}) collective-permute-start(bf16[1,4,64,128]{3,2,1,0:T(8,128)(2,1)S(1)} %collective-permute-done.7), channel_id=1, source_target_pairs={{224,0},{240,16},{0,32},{16,48},{32,64},{48,80},{64,96},{80,112},{... | collective-permute-start | bytes 196616 | tf_op jit(solution)/shard_map/ppermute | solution.py:20
  121.1 3.6 %collective-permute-done.15 = bf16[1,4,64,128]{3,2,1,0:T(8,128)(2,1)S(1)} collective-permute-done((bf16[1,4,64,128]{3,2,1,0:T(8,128)(2,1)S(1)}, bf16[1,4,64,128]{3,2,1,0:T(8,128)(2,1)S(1)}, u32[]{:S(2)}, u32[]{:S(2)}) %collective-permute-start.15) | collective-permute-done | bytes 65568 | tf_op jit(solution)/shard_map/ppermute | solution.py:20
  124.9 0.1 copy.75
  125.0 1.6 %scatter_fusion.1 = f32[4,64,128]{1,0,2:T(4,128)S(1)} fusion(f32[4,64,128]{1,0,2:T(4,128)S(1)} %copy.75, s32[32]{0:T(128)S(1)} %fusion.7, f32[32,4,64]{2,1,0:T(4,128)S(1)} %copy.76), kind=kCustom, calls=%fused_computation.4 | custom fusion | flops 8192 | bytes 98432 | tf_op jit(solution)/shard_map/scatter-add | solution.py:65
  126.7 1.6 %scatter_fusion.2 = f32[4,64,128]{1,0,2:T(4,128)S(1)} fusion(f32[4,64,128]{1,0,2:T(4,128)S(1)} %scatter_fusion.1, s32[32]{0:T(128)S(1)} %fusion.8, f32[32,4,64]{2,1,0:T(4,128)S(1)} %copy.77), kind=kCustom, calls=%fused_computation.5 | custom fusion | flops 8192 | bytes 98432 | tf_op jit(solution)/shard_map/scatter-add | solution.py:66
  128.4 0.7 copy.78
  129.1 0.7 fusion.5
  (47 shorter events, 1.4 us)
Async XLA Ops:
  0.6 33.5 %copy-start = (bf16[1,4,64,128]{3,2,1,0:T(8,128)(2,1)S(1)}, bf16[1,4,64,128]{3,2,1,0:T(8,128)(2,1)}, u32[]{:S(2)}) copy-start(bf16[1,4,64,128]{3,2,1,0:T(8,128)(2,1)} %param.10) | copy-start | bytes 196612
  0.6 33.5 %copy-start.1 = (s32[2,4,128]{2,1,0:T(4,128)S(1)}, s32[2,4,128]{2,1,0:T(4,128)}, u32[]{:S(2)}) copy-start(s32[2,4,128]{2,1,0:T(4,128)} %param.12) | copy-start | bytes 12292
  0.7 74.7 %collective-permute-start.2 = (bf16[1,4,64,128]{3,2,1,0:T(8,128)(2,1)}, bf16[1,4,64,128]{3,2,1,0:T(8,128)(2,1)S(1)}, u32[]{:S(2)}, u32[]{:S(2)}) collective-permute-start(bf16[1,4,64,128]{3,2,1,0:T(8,128)(2,1)} %param.9), channel_id=1, source_target_pairs={{224,0},{240,16},{0,32},{16,48},{32,64},{48,80},{64,96},{80,112},{... | collective-permute-start | bytes 196616 | tf_op jit(solution)/shard_map/ppermute | solution.py:20
  7.1 55.0 %collective-permute-start.1 = (bf16[1,4,64,32]{3,2,1,0:T(8,128)(2,1)}, bf16[1,4,64,32]{3,2,1,0:T(8,128)(2,1)S(1)}, u32[]{:S(2)}, u32[]{:S(2)}) collective-permute-start(bf16[1,4,64,32]{3,2,1,0:T(8,128)(2,1)} %bitcast_select_fusion.1), channel_id=1, source_target_pairs={{1,0},{2,1},{3,2},{4,3},{5,4},{6,5},{7,6},{8,7},{9,8},{10,9},{11,1... | collective-permute-start | bytes 49160 | tf_op jit(solution)/shard_map/ppermute | solution.py:14
  15.2 60.0 %collective-permute-start = (bf16[1,4,64,32]{3,2,1,0:T(8,128)(2,1)S(1)}, bf16[1,4,64,32]{3,2,1,0:T(8,128)(2,1)S(1)}, u32[]{:S(2)}, u32[]{:S(2)}) collective-permute-start(bf16[1,4,64,32]{3,2,1,0:T(8,128)(2,1)S(1)} %bitcast_select_fusion.2), channel_id=1, source_target_pairs={{0,1},{1,2},{2,3},{3,4},{4,5},{5,6},{6,7},{7,8},{8,9},{9,10},{10,1... | collective-permute-start | bytes 49160 | tf_op jit(solution)/shard_map/ppermute | solution.py:14
  17.1 54.1 %collective-permute-start.9 = (bf16[1,4,64,128]{3,2,1,0:T(8,128)(2,1)}, bf16[1,4,64,128]{3,2,1,0:T(8,128)(2,1)S(1)}, u32[]{:S(2)}, u32[]{:S(2)}) collective-permute-start(bf16[1,4,64,128]{3,2,1,0:T(8,128)(2,1)} %param.10), channel_id=1, source_target_pairs={{224,0},{240,16},{0,32},{16,48},{32,64},{48,80},{64,96},{80,112},{... | collective-permute-start | bytes 196616 | tf_op jit(solution)/shard_map/ppermute | solution.py:20
  34.3 26.9 %copy-start.2 = (s32[2,32]{1,0:T(2,128)S(1)}, s32[2,32]{1,0:T(2,128)}, u32[]{:S(2)}) copy-start(s32[2,32]{1,0:T(2,128)} %param.13) | copy-start | bytes 772
  34.3 26.9 %copy-start.3 = (s32[2,32]{1,0:T(2,128)S(1)}, s32[2,32]{1,0:T(2,128)}, u32[]{:S(2)}) copy-start(s32[2,32]{1,0:T(2,128)} %param.14) | copy-start | bytes 772
  59.2 49.1 %collective-permute-start.16 = (bf16[1,4,64,32]{3,2,1,0:T(8,128)(2,1)S(1)}, bf16[1,4,64,32]{3,2,1,0:T(8,128)(2,1)S(1)}, u32[]{:S(2)}, u32[]{:S(2)}) collective-permute-start(bf16[1,4,64,32]{3,2,1,0:T(8,128)(2,1)S(1)} %get-tuple-element.18), channel_id=1, source_target_pairs={{0,1},{1,2},{2,3},{3,4},{4,5},{5,6},{6,7},{7,8},{8,9},{9,10},{10,1... | collective-permute-start | bytes 49160 | tf_op jit(solution)/shard_map/ppermute | solution.py:14
  62.1 55.4 %collective-permute-start.17 = (bf16[1,4,64,32]{3,2,1,0:T(8,128)(2,1)S(1)}, bf16[1,4,64,32]{3,2,1,0:T(8,128)(2,1)S(1)}, u32[]{:S(2)}, u32[]{:S(2)}) collective-permute-start(bf16[1,4,64,32]{3,2,1,0:T(8,128)(2,1)S(1)} %get-tuple-element.17), channel_id=1, source_target_pairs={{1,0},{2,1},{3,2},{4,3},{5,4},{6,5},{7,6},{8,7},{9,8},{10,9},{11,1... | collective-permute-start | bytes 49160 | tf_op jit(solution)/shard_map/ppermute | solution.py:14
  71.2 7.7 %collective-permute-start.10 = (bf16[1,4,64,128]{3,2,1,0:T(8,128)(2,1)S(1)}, bf16[1,4,64,128]{3,2,1,0:T(8,128)(2,1)S(1)}, u32[]{:S(2)}, u32[]{:S(2)}) collective-permute-start(bf16[1,4,64,128]{3,2,1,0:T(8,128)(2,1)S(1)} %collective-permute-done.9), channel_id=1, source_target_pairs={{224,0},{240,16},{0,32},{16,48},{32,64},{48,80},{64,96},{80,112},{... | collective-permute-start | bytes 196616 | tf_op jit(solution)/shard_map/ppermute | solution.py:20
  75.4 9.8 %collective-permute-start.3 = (bf16[1,4,64,128]{3,2,1,0:T(8,128)(2,1)S(1)}, bf16[1,4,64,128]{3,2,1,0:T(8,128)(2,1)S(1)}, u32[]{:S(2)}, u32[]{:S(2)}) collective-permute-start(bf16[1,4,64,128]{3,2,1,0:T(8,128)(2,1)S(1)} %collective-permute-done.2), channel_id=1, source_target_pairs={{224,0},{240,16},{0,32},{16,48},{32,64},{48,80},{64,96},{80,112},{... | collective-permute-start | bytes 196616 | tf_op jit(solution)/shard_map/ppermute | solution.py:20
  78.9 8.5 %collective-permute-start.11 = (bf16[1,4,64,128]{3,2,1,0:T(8,128)(2,1)S(1)}, bf16[1,4,64,128]{3,2,1,0:T(8,128)(2,1)S(1)}, u32[]{:S(2)}, u32[]{:S(2)}) collective-permute-start(bf16[1,4,64,128]{3,2,1,0:T(8,128)(2,1)S(1)} %collective-permute-done.10), channel_id=1, source_target_pairs={{224,0},{240,16},{0,32},{16,48},{32,64},{48,80},{64,96},{80,112},{... | collective-permute-start | bytes 196616 | tf_op jit(solution)/shard_map/ppermute | solution.py:20
  85.2 10.0 %collective-permute-start.4 = (bf16[1,4,64,128]{3,2,1,0:T(8,128)(2,1)S(1)}, bf16[1,4,64,128]{3,2,1,0:T(8,128)(2,1)S(1)}, u32[]{:S(2)}, u32[]{:S(2)}) collective-permute-start(bf16[1,4,64,128]{3,2,1,0:T(8,128)(2,1)S(1)} %collective-permute-done.3), channel_id=1, source_target_pairs={{224,0},{240,16},{0,32},{16,48},{32,64},{48,80},{64,96},{80,112},{... | collective-permute-start | bytes 196616 | tf_op jit(solution)/shard_map/ppermute | solution.py:20
  87.4 8.5 %collective-permute-start.12 = (bf16[1,4,64,128]{3,2,1,0:T(8,128)(2,1)S(1)}, bf16[1,4,64,128]{3,2,1,0:T(8,128)(2,1)S(1)}, u32[]{:S(2)}, u32[]{:S(2)}) collective-permute-start(bf16[1,4,64,128]{3,2,1,0:T(8,128)(2,1)S(1)} %collective-permute-done.11), channel_id=1, source_target_pairs={{224,0},{240,16},{0,32},{16,48},{32,64},{48,80},{64,96},{80,112},{... | collective-permute-start | bytes 196616 | tf_op jit(solution)/shard_map/ppermute | solution.py:20
  95.2 8.4 %collective-permute-start.5 = (bf16[1,4,64,128]{3,2,1,0:T(8,128)(2,1)S(1)}, bf16[1,4,64,128]{3,2,1,0:T(8,128)(2,1)S(1)}, u32[]{:S(2)}, u32[]{:S(2)}) collective-permute-start(bf16[1,4,64,128]{3,2,1,0:T(8,128)(2,1)S(1)} %collective-permute-done.4), channel_id=1, source_target_pairs={{224,0},{240,16},{0,32},{16,48},{32,64},{48,80},{64,96},{80,112},{... | collective-permute-start | bytes 196616 | tf_op jit(solution)/shard_map/ppermute | solution.py:20
  95.9 12.3 %collective-permute-start.13 = (bf16[1,4,64,128]{3,2,1,0:T(8,128)(2,1)S(1)}, bf16[1,4,64,128]{3,2,1,0:T(8,128)(2,1)S(1)}, u32[]{:S(2)}, u32[]{:S(2)}) collective-permute-start(bf16[1,4,64,128]{3,2,1,0:T(8,128)(2,1)S(1)} %collective-permute-done.12), channel_id=1, source_target_pairs={{224,0},{240,16},{0,32},{16,48},{32,64},{48,80},{64,96},{80,112},{... | collective-permute-start | bytes 196616 | tf_op jit(solution)/shard_map/ppermute | solution.py:20
  103.6 8.8 %collective-permute-start.6 = (bf16[1,4,64,128]{3,2,1,0:T(8,128)(2,1)S(1)}, bf16[1,4,64,128]{3,2,1,0:T(8,128)(2,1)S(1)}, u32[]{:S(2)}, u32[]{:S(2)}) collective-permute-start(bf16[1,4,64,128]{3,2,1,0:T(8,128)(2,1)S(1)} %collective-permute-done.5), channel_id=1, source_target_pairs={{224,0},{240,16},{0,32},{16,48},{32,64},{48,80},{64,96},{80,112},{... | collective-permute-start | bytes 196616 | tf_op jit(solution)/shard_map/ppermute | solution.py:20
  108.2 9.3 %collective-permute-start.14 = (bf16[1,4,64,128]{3,2,1,0:T(8,128)(2,1)S(1)}, bf16[1,4,64,128]{3,2,1,0:T(8,128)(2,1)S(1)}, u32[]{:S(2)}, u32[]{:S(2)}) collective-permute-start(bf16[1,4,64,128]{3,2,1,0:T(8,128)(2,1)S(1)} %collective-permute-done.13), channel_id=1, source_target_pairs={{224,0},{240,16},{0,32},{16,48},{32,64},{48,80},{64,96},{80,112},{... | collective-permute-start | bytes 196616 | tf_op jit(solution)/shard_map/ppermute | solution.py:20
  112.4 7.3 %collective-permute-start.7 = (bf16[1,4,64,128]{3,2,1,0:T(8,128)(2,1)S(1)}, bf16[1,4,64,128]{3,2,1,0:T(8,128)(2,1)S(1)}, u32[]{:S(2)}, u32[]{:S(2)}) collective-permute-start(bf16[1,4,64,128]{3,2,1,0:T(8,128)(2,1)S(1)} %collective-permute-done.6), channel_id=1, source_target_pairs={{224,0},{240,16},{0,32},{16,48},{32,64},{48,80},{64,96},{80,112},{... | collective-permute-start | bytes 196616 | tf_op jit(solution)/shard_map/ppermute | solution.py:20
  117.5 7.3 %collective-permute-start.15 = (bf16[1,4,64,128]{3,2,1,0:T(8,128)(2,1)S(1)}, bf16[1,4,64,128]{3,2,1,0:T(8,128)(2,1)S(1)}, u32[]{:S(2)}, u32[]{:S(2)}) collective-permute-start(bf16[1,4,64,128]{3,2,1,0:T(8,128)(2,1)S(1)} %collective-permute-done.14), channel_id=1, source_target_pairs={{224,0},{240,16},{0,32},{16,48},{32,64},{48,80},{64,96},{80,112},{... | collective-permute-start | bytes 196616 | tf_op jit(solution)/shard_map/ppermute | solution.py:20
  119.7 9.4 %collective-permute-start.8 = (bf16[1,4,64,128]{3,2,1,0:T(8,128)(2,1)S(1)}, bf16[1,4,64,128]{3,2,1,0:T(8,128)(2,1)S(1)}, u32[]{:S(2)}, u32[]{:S(2)}) collective-permute-start(bf16[1,4,64,128]{3,2,1,0:T(8,128)(2,1)S(1)} %collective-permute-done.7), channel_id=1, source_target_pairs={{224,0},{240,16},{0,32},{16,48},{32,64},{48,80},{64,96},{80,112},{... | collective-permute-start | bytes 196616 | tf_op jit(solution)/shard_map/ppermute | solution.py:20
where the time goes:
time: 130 us
  starting transfers between devices  44.1 us (34%)
  local copies, waits for them, and re-layouts  24.4 us (19%)
  other arithmetic  23.5 us (18%)
  waiting for transfers between devices  23.2 us (18%)
  matrix products  13 us (10%)
  between operations  1.68 us (1%)
    ppermute x14, starting transfers between devices, from_behind(): return lax.ppermute(block, axis, route)  23.9 us
    ppermute x14, waiting for transfers between devices, from_behind(): return lax.ppermute(block, axis, route)  23.2 us
    ppermute x4, starting transfers between devices, passed_along(): lax.ppermute(value, axis, [(source, source + steps) for source in range(l...  20.2 us
    scatter-add x1, other arithmetic, body(): spread = jnp.zeros((groups, columns, block, width), jnp.float32).at[...,...  16.7 us
    another operation x3, local copies, waits for them, and re-layouts  16.1 us
    dot_general x1, matrix products, body(): jnp.einsum('ikabn,icbkn->ican', jacobian, stacked, preferred_element_type...  7.31 us
    dot_general x1, matrix products, body(): jnp.einsum('ikabn,ican->icbkn', jacobian, adjoint_in, preferred_element_t...  5.72 us
  transfers between devices with their start and end apart: 18, of which 9 were waited for; matrix products, arithmetic and copies ran while one was open for 46% of the time, Pallas kernels for 0%

commit v1 on v0

v1 whole, which is shorter than its diff:
```python
import math

import jax
import jax.numpy as jnp
from jax import lax
from jax.experimental import pallas as pl
from jax.experimental.pallas import tpu as pltpu
from jax.sharding import PartitionSpec as P

INST = 8
VMEM = pl.BlockSpec(memory_space=pltpu.VMEM)
SMEM = pl.BlockSpec(memory_space=pltpu.SMEM)
ANY = pl.BlockSpec(memory_space=pl.ANY)
HBM = pl.BlockSpec(memory_space=pltpu.HBM)


def coefficient(distance):
    parity = 1.0 - 2.0 * (distance % 2)
    return 0.5 * parity * math.cos(math.pi * distance / INST) / math.sin(math.pi * distance / INST)


def side_and_odd():
    sides = lax.axis_size("inst") // INST
    return lax.axis_index("inst") % sides, lax.axis_index("mesh") % 2


def picked_side(ref, side):
    return jnp.where(side == 0, ref[0], ref[1])


def send_matrix(low_ref, high_ref, columns, rows):
    side, odd = side_and_odd()
    low = jnp.where(side == 0, low_ref[0:1], low_ref[1:2])
    high = jnp.where(side == 0, high_ref[0:1], high_ref[1:2])
    first = jnp.where(odd == 1, low, high)
    second = jnp.where(odd == 1, high, low)
    places = [part + rows * c for part in (first, second) for c in range(columns)]
    target = jnp.concatenate(places, axis=1)
    at = lax.broadcasted_iota(jnp.int32, (columns * rows, target.shape[1]), 0)
    return (at == target).astype(jnp.float32).astype(jnp.bfloat16)


def neighbor_matrix(near_ref, rows, halo):
    side, odd = side_and_odd()
    near = picked_side(near_ref, side)
    swapped = jnp.where(near >= rows + halo, near - halo, near + halo)
    inside = near < rows
    outside = jnp.where(odd == 1, near, swapped)
    index = jnp.where(inside, near, jnp.where(near >= rows + 2 * halo, -1, outside))
    slots = near.shape[0]
    wide = jnp.concatenate([index[k : k + 1] for k in range(slots)], axis=1)
    at = lax.broadcasted_iota(jnp.int32, (2 * rows, slots * rows), 0)
    return (at == wide).astype(jnp.float32).astype(jnp.bfloat16)


def copied(pairs, sem):
    copies = [pltpu.make_async_copy(source, target, sem.at[i]) for i, (source, target) in enumerate(pairs)]
    for copy in copies:
        copy.start()
    return copies


def wait_all(copies):
    for copy in copies:
        copy.wait()


def pack_kernel(tangent_hbm, adjoint_hbm, chunks_ref, sem):
    wait_all(copied([(tangent_hbm, chunks_ref.at[:, 0]), (adjoint_hbm, chunks_ref.at[:, 1])], sem))


def adjoint_kernel(
    jac_hbm, adjoint_hbm, tangent_hbm, near_hbm, low_hbm, high_hbm, own_ref, first_ref, second_ref,
    jac_ref, sem, adjoint_ref, tangent_ref, near_ref, low_ref, high_ref, small_sem, weights, high, low
):
    small = copied(
        [
            (adjoint_hbm, adjoint_ref),
            (tangent_hbm, tangent_ref),
            (near_hbm, near_ref),
            (low_hbm, low_ref),
            (high_hbm, high_ref),
        ],
        small_sem,
    )
    columns, block, rows = adjoint_ref.shape[1:]
    slots = jac_ref.shape[0]
    halo = rows // columns
    copies = copied([(jac_hbm.at[0, k], jac_ref.at[k]) for k in range(slots)], sem)
    wait_all(small)
    rows_out = send_matrix(low_ref, high_ref, columns, rows)
    wide = jnp.concatenate([tangent_ref[0, c] for c in range(columns)], axis=1)
    out = jnp.dot(wide, rows_out, preferred_element_type=jnp.float32).astype(jnp.bfloat16)
    first_ref[:block] = out[:, :rows]
    second_ref[:block] = out[:, rows:]
    for c in range(columns):
        weights[c] = adjoint_ref[0, c].astype(jnp.float32)

    def one_slot(k, keep):
        def step(a, acc):
            jac = jac_ref[k, a].astype(jnp.float32)
            return tuple(acc[c] + jac * weights[c, pl.ds(a, 1), :] for c in range(columns))

        zero = tuple(jnp.zeros((block, rows), jnp.float32) for _ in range(columns))
        acc = lax.fori_loop(0, block, step, zero, unroll=8)
        for c in range(columns):
            keep(c, acc[c])

    def keep_own(c, value):
        own_ref[c] = value

    copies[0].wait()
    one_slot(0, keep_own)

    def other_slot(k, carry):
        def keep(c, value):
            top = value.astype(jnp.bfloat16)
            at = pl.ds(pl.multiple_of((k - 1) * rows, rows), rows)
            high[c, :, at] = top
            low[c, :, at] = (value - top.astype(jnp.float32)).astype(jnp.bfloat16)

        pltpu.make_async_copy(jac_hbm.at[0, k], jac_ref.at[k], sem.at[k]).wait()
        one_slot(k, keep)
        return carry

    lax.fori_loop(1, slots, other_slot, 0)
    matrix = neighbor_matrix(near_ref, rows, halo)
    transposed = (((1,), (1,)), ((), ()))
    lane = lax.broadcasted_iota(jnp.int32, (block, rows), 1)
    first = jnp.zeros((block, rows), jnp.float32)
    second = jnp.zeros((block, rows), jnp.float32)
    for c in range(columns):
        q = lax.dot_general(high[c], matrix, transposed, preferred_element_type=jnp.float32)
        q = q + lax.dot_general(low[c], matrix, transposed, preferred_element_type=jnp.float32)
        own_ref[c] = own_ref[c] + q[:, :rows]
        edge = q[:, rows:]
        here = lane // halo == c
        first = jnp.where(here, pltpu.roll(edge, (halo * c) % rows, 1), first)
        second = jnp.where(here, pltpu.roll(edge, (halo * c - halo) % rows, 1), second)
    first_ref[block:] = first.astype(jnp.bfloat16)
    second_ref[block:] = second.astype(jnp.bfloat16)


def tangent_kernel(
    jac_hbm, tangent_hbm, near_hbm, low_hbm, high_hbm, first_ref, second_ref, own_ref, mixed_ref, image_ref, sum_ref,
    jac_ref, sem, tangent_ref, near_ref, low_ref, high_ref, small_sem, picked, partial
):
    small = copied(
        [(tangent_hbm, tangent_ref), (near_hbm, near_ref), (low_hbm, low_ref), (high_hbm, high_ref)], small_sem
    )
    columns, block, rows = tangent_ref.shape[1:]
    slots = jac_ref.shape[0]
    halo = rows // columns
    group = 4
    deep = 16
    loads = sem.shape[0]
    load = block // loads
    parts = [pl.ds(part * load, load) for part in range(loads)]
    copies = copied([(jac_hbm.at[0, :, at], jac_ref.at[:, at]) for at in parts], sem)
    wait_all(small)
    matrix = neighbor_matrix(near_ref, rows, halo)
    lane = lax.broadcasted_iota(jnp.int32, (block, rows), 1)
    first = first_ref[:block].astype(jnp.float32)
    second = second_ref[:block].astype(jnp.float32)
    for c in range(columns):
        edge = jnp.where(
            lane < halo,
            pltpu.roll(first, (rows - halo * c) % rows, 1),
            pltpu.roll(second, (rows + halo - halo * c) % rows, 1),
        ).astype(jnp.bfloat16)
        own = tangent_ref[0, c]
        wide = jnp.dot(jnp.concatenate([own, edge], axis=1), matrix, preferred_element_type=jnp.float32)
        picked[c, :block] = own.astype(jnp.float32)
        for k in range(slots - 1):
            picked[c, (k + 1) * block : (k + 2) * block] = wide[:, k * rows : (k + 1) * rows]

    def one_group(g, carry):
        acc = [[jnp.zeros((8, rows), jnp.float32) for _ in range(columns)] for _ in range(group)]
        for k in range(slots):
            for b in range(0, block, deep):
                x = [picked[c, k * block + b : k * block + b + deep] for c in range(columns)]
                for a in range(group):
                    jac = jac_ref[k, g * group + a, b : b + deep, :].astype(jnp.float32)
                    for c in range(columns):
                        product = jac * x[c]
                        acc[a][c] = acc[a][c] + product[:8] + product[8:]
        for a in range(group):
            for c in range(columns):
                at = pl.multiple_of((c * block + g * group + a) * 8, 8)
                partial[pl.ds(at, 8), :] = acc[a][c]
        return carry

    per = load // group
    for part in range(loads):
        copies[part].wait()
        lax.fori_loop(part * per, (part + 1) * per, one_group, 0)
    for c in range(columns):
        for a in range(0, block, 8):
            base = (c * block + a) * 8
            total = partial[pl.ds(base, 8, stride=8), :]
            for s in range(1, 8):
                total = total + partial[pl.ds(base + s, 8, stride=8), :]
            image_ref[c, a : a + 8] = total
    back = jnp.concatenate([first_ref[block:], second_ref[block:]], axis=1)
    out = send_matrix(low_ref, high_ref, columns, rows)
    added = lax.dot_general(back, out, (((1,), (1,)), ((), ())), preferred_element_type=jnp.float32)
    for c in range(columns):
        sum_ref[c] = own_ref[c] + added[:, c * rows : (c + 1) * rows]


def mix_kernel(frequency_ref, chunks_ref, after_ref, mixed_ref):
    count = chunks_ref.shape[0]
    frequency = frequency_ref[0]
    for panel, sign in ((0, 1.0), (1, -1.0)):
        x = [chunks_ref[j, panel].astype(jnp.float32) for j in range(count)]
        for i in range(count):
            total = None
            for j in range(count):
                if i != j:
                    term = (coefficient((i - j) % count) * sign) * x[j]
                    total = term if total is None else total + term
            mixed_ref[i, panel] = (total * frequency).astype(jnp.bfloat16)


def last_kernel(image_ref, sum_ref, mixed_ref, tangent_ref, adjoint_ref):
    for out_ref, part_ref, panel in ((tangent_ref, image_ref, 0), (adjoint_ref, sum_ref, 1)):
        out_ref[...] = (part_ref[...] + mixed_ref[:, panel].astype(jnp.float32)).astype(jnp.bfloat16)


def call(kernel, out, inputs, specs, scratch=(), flops=0, bytes_accessed=0):
    return pl.pallas_call(
        kernel,
        out_shape=out,
        in_specs=specs,
        out_specs=jax.tree.map(lambda _: VMEM, out),
        scratch_shapes=list(scratch),
        cost_estimate=pl.CostEstimate(flops=flops, bytes_accessed=bytes_accessed, transcendentals=0),
        compiler_params=pltpu.CompilerParams(vmem_limit_bytes=40 << 20),
    )(*inputs)


def body(tangent_in, adjoint_in, jacobian, neighbors, send_low, send_high, frequency):
    _, columns, block, rows = tangent_in.shape
    slots = jacobian.shape[1]
    sides = lax.axis_size("inst") // INST
    mesh_size = lax.axis_size("mesh")
    slabs = sides * mesh_size
    groups = [[side + sides * i for i in range(INST)] for side in range(sides)]

    def device(instance, slab):
        return (instance * sides + slab // mesh_size) * mesh_size + slab % mesh_size

    def pairs(start):
        found = []
        for instance in range(INST):
            for slab in range(start, slabs - 1, 2):
                low, high = device(instance, slab), device(instance, slab + 1)
                found += [(low, high), (high, low)]
        return found

    def exchanged(first, second):
        second = lax.ppermute(second, ("inst", "mesh"), pairs(1))
        first = lax.ppermute(first, ("inst", "mesh"), pairs(0))
        return first, second

    def swapped(chunks):
        return lax.all_to_all(chunks, "inst", 0, 0, axis_index_groups=groups, tiled=True)

    f32, b16 = jnp.float32, jnp.bfloat16
    shape = jax.ShapeDtypeStruct
    chunk = shape((INST, 2, columns * block // INST, rows), b16)
    edge = shape((2 * block, rows), b16)
    panel = shape((columns, block, rows), f32)
    loaded = pltpu.VMEM((slots, block, block, rows), b16)
    dma = pltpu.SemaphoreType.DMA
    copy_of = lambda array: pltpu.VMEM(array.shape, array.dtype)
    split = lambda array: array.reshape((INST, columns * block // INST, rows))
    chunks = call(pack_kernel, chunk, (split(tangent_in), split(adjoint_in)), [HBM] * 2, [dma((2,))], bytes_accessed=1 << 19)
    chunks = swapped(chunks)
    small = (adjoint_in, tangent_in, neighbors, send_low, send_high)
    own, first, second = call(
        adjoint_kernel,
        (panel, edge, edge),
        (jacobian, *small),
        [HBM] * 6,
        [
            loaded,
            dma((slots,)),
            *map(copy_of, small),
            dma((len(small),)),
            pltpu.VMEM((columns, block, rows), f32),
            pltpu.VMEM((columns, block, (slots - 1) * rows), b16),
            pltpu.VMEM((columns, block, (slots - 1) * rows), b16),
        ],
        flops=1 << 32,
        bytes_accessed=6 << 20,
    )
    first, second = exchanged(first, second)
    mixed = call(mix_kernel, chunk, (frequency, chunks, own), [SMEM, VMEM, ANY], bytes_accessed=1 << 19)
    back = swapped(mixed)
    small = small[1:]
    image, total = call(
        tangent_kernel,
        (panel, panel),
        (jacobian, *small, first, second, own, mixed),
        [HBM] * 5 + [VMEM] * 3 + [ANY],
        [
            loaded,
            dma((4,)),
            *map(copy_of, small),
            dma((len(small),)),
            pltpu.VMEM((columns, slots * block, rows), f32),
            pltpu.VMEM((columns * block * 8, rows), f32),
        ],
        flops=1 << 32,
        bytes_accessed=6 << 20,
    )
    out = shape((INST, columns * block // INST, rows), b16)
    tangent_out, adjoint_out = call(last_kernel, (out, out), (split(image), split(total), back), [VMEM] * 3, bytes_accessed=1 << 19)
    return tangent_out.reshape(tangent_in.shape), adjoint_out.reshape(tangent_in.shape)


def solution(mesh):
    in_specs = (
        P("inst", None, None, "mesh"),
        P("inst", None, None, "mesh"),
        P("inst", None, None, None, "mesh"),
        P(None, None, "mesh"),
        P(None, "mesh"),
        P(None, "mesh"),
        P(),
    )
    out_specs = (P("inst", None, None, "mesh"), P("inst", None, None, "mesh"))
    return jax.shard_map(body, mesh=mesh, in_specs=in_specs, out_specs=out_specs, check_vma=False)
```

time: 130 us -> 50.3 us (0.39)
  the two profiles are of different devices: /device:TPU:2 before, /device:TPU:32 now
where the time goes in v1:
time: 50.3 us; the launch traced here: 49.7 us
  starting transfers between devices  23.7 us (47%)
  Pallas kernels  12 us (24%)
  local copies, waits for them, and re-layouts  10.4 us (21%)
  waiting for transfers between devices  2.25 us (4%)
  between operations  1.4 us (3%)
    all_to_all x2, starting transfers between devices, swapped(): lax.all_to_all(chunks, 'inst', 0, 0, axis_index_groups=groups, tiled=True)  16 us
    pallas_call x5, Pallas kernels, call(): pl.pallas_call(kernel, out_shape=out, in_specs=specs, out_specs=jax.tree....  12 us
    unnamed x26, local copies, waits for them, and re-layouts  10.4 us
    ppermute x1, starting transfers between devices, exchanged(): second = lax.ppermute(second, ('inst', 'mesh'), pairs(1))  7.62 us
    all_to_all x2, waiting for transfers between devices, swapped(): lax.all_to_all(chunks, 'inst', 0, 0, axis_index_groups=groups, tiled=True)  2.24 us
  transfers between devices with their start and end apart: 4, of which 1 were waited for; matrix products, arithmetic and copies ran while one was open for 0% of the time, Pallas kernels for 21%

profile of v1, /device:TPU:32, one launch (start us, length us, event | category | flops | bytes accessed | tf_op | source)
XLA Modules:
  0.0 49.7 jit_solution(14078892414937305354)
XLA Ops:
  0.6 0.0 copy-start
  0.6 0.8 %copy-done = bf16[1,4,64,128]{3,2,1,0:T(8,128)(2,1)S(1)} copy-done((bf16[1,4,64,128]{3,2,1,0:T(8,128)(2,1)S(1)}, bf16[1,4,64,128]{3,2,1,0:T(8,128)(2,1)}, u32[]{:S(2)}) %copy-start) | copy-done | bytes 65560
  1.5 0.0 copy-start.2
  1.5 0.8 %copy-done.2 = bf16[1,4,64,128]{3,2,1,0:T(8,128)(2,1)S(1)} copy-done((bf16[1,4,64,128]{3,2,1,0:T(8,128)(2,1)S(1)}, bf16[1,4,64,128]{3,2,1,0:T(8,128)(2,1)}, u32[]{:S(2)}) %copy-start.2) | copy-done | bytes 65560
  2.3 0.7 %shard_map.87 = bf16[8,2,32,128]{3,2,1,0:T(8,128)(2,1)} custom-call(bf16[8,32,128]{2,1,0:T(8,128)(2,1)S(1)} %bitcast.9, bf16[8,32,128]{2,1,0:T(8,128)(2,1)S(1)} %bitcast.8), custom_call_target="tpu_custom_call" | custom-call | bytes 524288 | tf_op jit(solution)/shard_map/pallas_call | solution.py:231
  3.0 8.5 %all-to-all-start = ((bf16[8,2,32,128]{3,2,1,0:T(8,128)(2,1)}), bf16[8,2,32,128]{3,2,1,0:T(8,128)(2,1)S(1)}, u32[]{:S(2)}, u32[]{:S(2)}) async-start(bf16[8,2,32,128]{3,2,1,0:T(8,128)(2,1)} %shard_map.87), calls=%async_computation | async-start | bytes 262144 | tf_op jit(solution)/shard_map/all_to_all | solution.py:267
  11.5 0.0 copy-start.1
  11.5 0.8 %copy-done.1 = bf16[1,4,64,128]{3,2,1,0:T(8,128)(2,1)S(1)} copy-done((bf16[1,4,64,128]{3,2,1,0:T(8,128)(2,1)S(1)}, bf16[1,4,64,128]{3,2,1,0:T(8,128)(2,1)}, u32[]{:S(2)}) %copy-start.1) | copy-done | bytes 65560
  12.3 0.0 copy-start.3
  12.3 0.8 %copy-done.3 = bf16[1,4,64,128]{3,2,1,0:T(8,128)(2,1)S(1)} copy-done((bf16[1,4,64,128]{3,2,1,0:T(8,128)(2,1)S(1)}, bf16[1,4,64,128]{3,2,1,0:T(8,128)(2,1)}, u32[]{:S(2)}) %copy-start.3) | copy-done | bytes 65560
  13.2 0.0 copy-start.5
  13.2 2.5 %copy-done.5 = bf16[1,5,64,64,128]{4,3,2,1,0:T(8,128)(2,1)S(1)} copy-done((bf16[1,5,64,64,128]{4,3,2,1,0:T(8,128)(2,1)S(1)}, bf16[1,5,64,64,128]{4,3,2,1,0:T(8,128)(2,1)}, u32[]{:S(2)}) %copy-start.5) | copy-done | bytes 5242904
  15.7 0.0 copy-start.7
  15.7 0.7 %copy-done.7 = s32[2,4,128]{2,1,0:T(4,128)S(1)} copy-done((s32[2,4,128]{2,1,0:T(4,128)S(1)}, s32[2,4,128]{2,1,0:T(4,128)}, u32[]{:S(2)}) %copy-start.7) | copy-done | bytes 4120
  16.4 0.0 copy-start.9
  16.4 0.7 %copy-done.9 = s32[2,32]{1,0:T(2,128)S(1)} copy-done((s32[2,32]{1,0:T(2,128)S(1)}, s32[2,32]{1,0:T(2,128)}, u32[]{:S(2)}) %copy-start.9) | copy-done | bytes 280
  17.0 0.0 copy-start.11
  17.0 0.7 %copy-done.11 = s32[2,32]{1,0:T(2,128)S(1)} copy-done((s32[2,32]{1,0:T(2,128)S(1)}, s32[2,32]{1,0:T(2,128)}, u32[]{:S(2)}) %copy-start.11) | copy-done | bytes 280
  17.7 0.0 copy-start.4
  17.7 0.0 copy-start.8
  17.7 0.0 copy-start.10
  17.7 0.0 copy-start.12
  17.7 5.3 %shard_map.86 = (f32[4,64,128]{2,1,0:T(8,128)S(1)}, bf16[128,128]{1,0:T(8,128)(2,1)S(1)}, bf16[128,128]{1,0:T(8,128)(2,1)S(1)}) custom-call(bf16[1,5,64,64,128]{4,3,2,1,0:T(8,128)(2,1)S(1)} %copy-done.5, bf16[1,4,64,128]{3,2,1,0:T(8,128)(2,1)S(1)} %copy-done.1, bf16[1,4,64,128]{3,2,1,0:T(8,128)(2,1)S(1)} %copy-done.3, s32[2,4,128]{2,1,0:T(4,128)S(1)} %copy-done.7, ...), custom_call_target="tpu_custom_call" | custom-call | flops 4294967296 | bytes 6291456 | tf_op jit(solution)/shard_map/pallas_call | solution.py:231
  23.0 0.1 collective-permute-start
  23.1 7.6 %collective-permute-start.1 = (bf16[128,128]{1,0:T(8,128)(2,1)S(1)}, bf16[128,128]{1,0:T(8,128)(2,1)S(1)}, u32[]{:S(2)}, u32[]{:S(2)}) collective-permute-start(bf16[128,128]{1,0:T(8,128)(2,1)S(1)} %get-tuple-element.10), channel_id=1, source_target_pairs={{1,2},{2,1},{3,4},{4,3},{5,6},{6,5},{7,8},{8,7},{9,10},{10,9},{11,... | collective-permute-start | bytes 98312 | tf_op jit(solution)/shard_map/ppermute | solution.py:262
  31.4 0.0 all-to-all-done.chunks_ref
  31.4 0.8 %shard_map.88.mixed_ref = bf16[8,2,32,128]{3,2,1,0:T(8,128)(2,1)} custom-call(f32[1]{0:T(128)S(6)} %copy.9.frequency_ref, bf16[8,2,32,128]{3,2,1,0:T(8,128)(2,1)S(1)} %all-to-all-done.chunks_ref, f32[4,64,128]{2,1,0:T(8,128)S(1)} %get-tuple-element.11.after_ref.own_ref), custom_call_target="tpu_custom_call" | custom-call | bytes 524288 | tf_op jit(solution)/shard_map/pallas_call | solution.py:231
  32.2 7.5 %all-to-all-start.1 = ((bf16[8,2,32,128]{3,2,1,0:T(8,128)(2,1)}), bf16[8,2,32,128]{3,2,1,0:T(8,128)(2,1)S(1)}, u32[]{:S(2)}, u32[]{:S(2)}) async-start(bf16[8,2,32,128]{3,2,1,0:T(8,128)(2,1)} %shard_map.88.mixed_ref), calls=%async_computation.1 | async-start | bytes 262144 | tf_op jit(solution)/shard_map/all_to_all | solution.py:267
  39.7 0.0 collective-permute-done.first_ref
  39.7 0.0 collective-permute-done.1.second_ref
  39.7 0.0 copy-done.4
  39.7 0.0 copy-done.8
  39.7 0.0 copy-done.10
  39.7 0.0 copy-done.12
  39.7 0.0 copy-start.6
  39.7 2.5 %copy-done.6 = bf16[1,5,64,64,128]{4,3,2,1,0:T(8,128)(2,1)S(1)} copy-done((bf16[1,5,64,64,128]{4,3,2,1,0:T(8,128)(2,1)S(1)}, bf16[1,5,64,64,128]{4,3,2,1,0:T(8,128)(2,1)}, u32[]{:S(2)}) %copy-start.6) | copy-done | bytes 5242904
  42.2 4.6 %shard_map.89 = (f32[4,64,128]{2,1,0:T(8,128)S(1)}, f32[4,64,128]{2,1,0:T(8,128)S(1)}) custom-call(bf16[1,5,64,64,128]{4,3,2,1,0:T(8,128)(2,1)S(1)} %copy-done.6, bf16[1,4,64,128]{3,2,1,0:T(8,128)(2,1)S(1)} %copy-done.4, s32[2,4,128]{2,1,0:T(4,128)S(1)} %copy-done.8, s32[2,32]{1,0:T(2,128)S(1)} %copy-done.10, s32[2,32]{1,0:T(2,128)S(1)} %copy-done.12, ...), custom_call_target="tpu_custom_call" | custom-call | flops 4294967296 | bytes 6291456 | tf_op jit(solution)/shard_map/pallas_call | solution.py:231
  46.8 2.2 %all-to-all-done.1.mixed_ref = bf16[8,2,32,128]{3,2,1,0:T(8,128)(2,1)S(1)} async-done(((bf16[8,2,32,128]{3,2,1,0:T(8,128)(2,1)}), bf16[8,2,32,128]{3,2,1,0:T(8,128)(2,1)S(1)}, u32[]{:S(2)}, u32[]{:S(2)}) %all-to-all-start.1) | async-done | bytes 131104 | tf_op jit(solution)/shard_map/all_to_all | solution.py:267
  49.1 0.7 %shard_map.90 = (bf16[8,32,128]{2,1,0:T(8,128)(2,1)}, bf16[8,32,128]{2,1,0:T(8,128)(2,1)}) custom-call(f32[8,32,128]{2,1,0:T(8,128)S(1)} %bitcast.6, f32[8,32,128]{2,1,0:T(8,128)S(1)} %bitcast.7, bf16[8,2,32,128]{3,2,1,0:T(8,128)(2,1)S(1)} %all-to-all-done.1.mixed_ref), custom_call_target="tpu_custom_call" | custom-call | bytes 524288 | tf_op jit(solution)/shard_map/pallas_call | solution.py:231
Async XLA Ops:
  0.6 0.8 %copy-start = (bf16[1,4,64,128]{3,2,1,0:T(8,128)(2,1)S(1)}, bf16[1,4,64,128]{3,2,1,0:T(8,128)(2,1)}, u32[]{:S(2)}) copy-start(bf16[1,4,64,128]{3,2,1,0:T(8,128)(2,1)} %adjoint_hbm.1) | copy-start | bytes 196612
  1.5 0.8 %copy-start.2 = (bf16[1,4,64,128]{3,2,1,0:T(8,128)(2,1)S(1)}, bf16[1,4,64,128]{3,2,1,0:T(8,128)(2,1)}, u32[]{:S(2)}) copy-start(bf16[1,4,64,128]{3,2,1,0:T(8,128)(2,1)} %tangent_hbm.3) | copy-start | bytes 196612
  3.0 28.4 %all-to-all-start = ((bf16[8,2,32,128]{3,2,1,0:T(8,128)(2,1)}), bf16[8,2,32,128]{3,2,1,0:T(8,128)(2,1)S(1)}, u32[]{:S(2)}, u32[]{:S(2)}) async-start(bf16[8,2,32,128]{3,2,1,0:T(8,128)(2,1)} %shard_map.87), calls=%async_computation | async-start | bytes 262144 | tf_op jit(solution)/shard_map/all_to_all | solution.py:267
  11.5 0.8 %copy-start.1 = (bf16[1,4,64,128]{3,2,1,0:T(8,128)(2,1)S(1)}, bf16[1,4,64,128]{3,2,1,0:T(8,128)(2,1)}, u32[]{:S(2)}) copy-start(bf16[1,4,64,128]{3,2,1,0:T(8,128)(2,1)} %adjoint_hbm.1) | copy-start | bytes 196612
  12.3 0.8 %copy-start.3 = (bf16[1,4,64,128]{3,2,1,0:T(8,128)(2,1)S(1)}, bf16[1,4,64,128]{3,2,1,0:T(8,128)(2,1)}, u32[]{:S(2)}) copy-start(bf16[1,4,64,128]{3,2,1,0:T(8,128)(2,1)} %tangent_hbm.3) | copy-start | bytes 196612
  13.2 2.5 %copy-start.5 = (bf16[1,5,64,64,128]{4,3,2,1,0:T(8,128)(2,1)S(1)}, bf16[1,5,64,64,128]{4,3,2,1,0:T(8,128)(2,1)}, u32[]{:S(2)}) copy-start(bf16[1,5,64,64,128]{4,3,2,1,0:T(8,128)(2,1)} %jac_hbm.3) | copy-start | bytes 15728644
  15.7 0.7 %copy-start.7 = (s32[2,4,128]{2,1,0:T(4,128)S(1)}, s32[2,4,128]{2,1,0:T(4,128)}, u32[]{:S(2)}) copy-start(s32[2,4,128]{2,1,0:T(4,128)} %near_hbm.3) | copy-start | bytes 12292
  16.4 0.7 %copy-start.9 = (s32[2,32]{1,0:T(2,128)S(1)}, s32[2,32]{1,0:T(2,128)}, u32[]{:S(2)}) copy-start(s32[2,32]{1,0:T(2,128)} %low_hbm.3) | copy-start | bytes 772
  17.0 0.7 %copy-start.11 = (s32[2,32]{1,0:T(2,128)S(1)}, s32[2,32]{1,0:T(2,128)}, u32[]{:S(2)}) copy-start(s32[2,32]{1,0:T(2,128)} %high_hbm.3) | copy-start | bytes 772
  17.7 22.0 %copy-start.4 = (bf16[1,4,64,128]{3,2,1,0:T(8,128)(2,1)S(1)}, bf16[1,4,64,128]{3,2,1,0:T(8,128)(2,1)}, u32[]{:S(2)}) copy-start(bf16[1,4,64,128]{3,2,1,0:T(8,128)(2,1)} %tangent_hbm.3) | copy-start | bytes 196612
  17.7 22.0 %copy-start.8 = (s32[2,4,128]{2,1,0:T(4,128)S(1)}, s32[2,4,128]{2,1,0:T(4,128)}, u32[]{:S(2)}) copy-start(s32[2,4,128]{2,1,0:T(4,128)} %near_hbm.3) | copy-start | bytes 12292
  17.7 22.0 %copy-start.10 = (s32[2,32]{1,0:T(2,128)S(1)}, s32[2,32]{1,0:T(2,128)}, u32[]{:S(2)}) copy-start(s32[2,32]{1,0:T(2,128)} %low_hbm.3) | copy-start | bytes 772
  17.7 22.0 %copy-start.12 = (s32[2,32]{1,0:T(2,128)S(1)}, s32[2,32]{1,0:T(2,128)}, u32[]{:S(2)}) copy-start(s32[2,32]{1,0:T(2,128)} %high_hbm.3) | copy-start | bytes 772
  23.0 16.7 %collective-permute-start = (bf16[128,128]{1,0:T(8,128)(2,1)S(1)}, bf16[128,128]{1,0:T(8,128)(2,1)S(1)}, u32[]{:S(2)}, u32[]{:S(2)}) collective-permute-start(bf16[128,128]{1,0:T(8,128)(2,1)S(1)} %get-tuple-element.9), channel_id=1, source_target_pairs={{0,1},{1,0},{2,3},{3,2},{4,5},{5,4},{6,7},{7,6},{8,9},{9,8},{10,11... | collective-permute-start | bytes 98312 | tf_op jit(solution)/shard_map/ppermute | solution.py:263
  23.1 16.6 %collective-permute-start.1 = (bf16[128,128]{1,0:T(8,128)(2,1)S(1)}, bf16[128,128]{1,0:T(8,128)(2,1)S(1)}, u32[]{:S(2)}, u32[]{:S(2)}) collective-permute-start(bf16[128,128]{1,0:T(8,128)(2,1)S(1)} %get-tuple-element.10), channel_id=1, source_target_pairs={{1,2},{2,1},{3,4},{4,3},{5,6},{6,5},{7,8},{8,7},{9,10},{10,9},{11,... | collective-permute-start | bytes 98312 | tf_op jit(solution)/shard_map/ppermute | solution.py:262
  32.2 16.9 %all-to-all-start.1 = ((bf16[8,2,32,128]{3,2,1,0:T(8,128)(2,1)}), bf16[8,2,32,128]{3,2,1,0:T(8,128)(2,1)S(1)}, u32[]{:S(2)}, u32[]{:S(2)}) async-start(bf16[8,2,32,128]{3,2,1,0:T(8,128)(2,1)} %shard_map.88.mixed_ref), calls=%async_computation.1 | async-start | bytes 262144 | tf_op jit(solution)/shard_map/all_to_all | solution.py:267
  39.7 2.5 %copy-start.6 = (bf16[1,5,64,64,128]{4,3,2,1,0:T(8,128)(2,1)S(1)}, bf16[1,5,64,64,128]{4,3,2,1,0:T(8,128)(2,1)}, u32[]{:S(2)}) copy-start(bf16[1,5,64,64,128]{4,3,2,1,0:T(8,128)(2,1)} %jac_hbm.3) | copy-start | bytes 15728644

commit v2 on v1

--- a/solution.py
+++ b/solution.py
@@ -8,15 +8,20 @@
 from jax.sharding import PartitionSpec as P
 
 INST = 8
+HALF = INST // 2
 VMEM = pl.BlockSpec(memory_space=pltpu.VMEM)
 SMEM = pl.BlockSpec(memory_space=pltpu.SMEM)
 ANY = pl.BlockSpec(memory_space=pl.ANY)
-HBM = pl.BlockSpec(memory_space=pltpu.HBM)
 
 
 def coefficient(distance):
     parity = 1.0 - 2.0 * (distance % 2)
     return 0.5 * parity * math.cos(math.pi * distance / INST) / math.sin(math.pi * distance / INST)
+
+
+def place():
+    instance = lax.axis_index("inst") // (lax.axis_size("inst") // INST)
+    return instance // HALF, instance % HALF
 
 
 def side_and_odd():
@@ -60,34 +65,27 @@
     return copies
 
 
-def wait_all(copies):
-    for copy in copies:
-        copy.wait()
-
-
-def pack_kernel(tangent_hbm, adjoint_hbm, chunks_ref, sem):
-    wait_all(copied([(tangent_hbm, chunks_ref.at[:, 0]), (adjoint_hbm, chunks_ref.at[:, 1])], sem))
+def half_kernel(half_ref):
+    half_ref[...] = jnp.full(half_ref.shape, place()[0], jnp.int32)
+
+
+def pair_kernel(tangent_ref, adjoint_ref, partner_ref, after_ref, pair_ref, difference_ref):
+    upper = place()[0] == 1
+    mine = jnp.where(upper, adjoint_ref[0], tangent_ref[0])
+    other = partner_ref[0]
+    first, second = jnp.where(upper, other, mine), jnp.where(upper, mine, other)
+    pair_ref[0], pair_ref[1] = first, second
+    difference_ref[...] = (first.astype(jnp.float32) - second.astype(jnp.float32)).astype(jnp.bfloat16)
 
 
 def adjoint_kernel(
-    jac_hbm, adjoint_hbm, tangent_hbm, near_hbm, low_hbm, high_hbm, own_ref, first_ref, second_ref,
-    jac_ref, sem, adjoint_ref, tangent_ref, near_ref, low_ref, high_ref, small_sem, weights, high, low
+    jac_hbm, adjoint_ref, tangent_ref, near_ref, low_ref, high_ref, own_ref, first_ref, second_ref,
+    jac_ref, sem, weights, high, low
 ):
-    small = copied(
-        [
-            (adjoint_hbm, adjoint_ref),
-            (tangent_hbm, tangent_ref),
-            (near_hbm, near_ref),
-            (low_hbm, low_ref),
-            (high_hbm, high_ref),
-        ],
-        small_sem,
-    )
     columns, block, rows = adjoint_ref.shape[1:]
     slots = jac_ref.shape[0]
     halo = rows // columns
     copies = copied([(jac_hbm.at[0, k], jac_ref.at[k]) for k in range(slots)], sem)
-    wait_all(small)
     rows_out = send_matrix(low_ref, high_ref, columns, rows)
     wide = jnp.concatenate([tangent_ref[0, c] for c in range(columns)], axis=1)
     out = jnp.dot(wide, rows_out, preferred_element_type=jnp.float32).astype(jnp.bfloat16)
@@ -142,12 +140,9 @@
 
 
 def tangent_kernel(
-    jac_hbm, tangent_hbm, near_hbm, low_hbm, high_hbm, first_ref, second_ref, own_ref, mixed_ref, image_ref, sum_ref,
-    jac_ref, sem, tangent_ref, near_ref, low_ref, high_ref, small_sem, picked, partial
+    jac_hbm, tangent_ref, near_ref, low_ref, high_ref, first_ref, second_ref, own_ref, mixed_ref, image_ref, sum_ref,
+    jac_ref, sem, picked, partial
 ):
-    small = copied(
-        [(tangent_hbm, tangent_ref), (near_hbm, near_ref), (low_hbm, low_ref), (high_hbm, high_ref)], small_sem
-    )
     columns, block, rows = tangent_ref.shape[1:]
     slots = jac_ref.shape[0]
     halo = rows // columns
@@ -157,7 +152,6 @@
     load = block // loads
     parts = [pl.ds(part * load, load) for part in range(loads)]
     copies = copied([(jac_hbm.at[0, :, at], jac_ref.at[:, at]) for at in parts], sem)
-    wait_all(small)
     matrix = neighbor_matrix(near_ref, rows, halo)
     lane = lax.broadcasted_iota(jnp.int32, (block, rows), 1)
     first = first_ref[:block].astype(jnp.float32)
@@ -208,23 +202,40 @@
         sum_ref[c] = own_ref[c] + added[:, c * rows : (c + 1) * rows]
 
 
-def mix_kernel(frequency_ref, chunks_ref, after_ref, mixed_ref):
-    count = chunks_ref.shape[0]
-    frequency = frequency_ref[0]
-    for panel, sign in ((0, 1.0), (1, -1.0)):
-        x = [chunks_ref[j, panel].astype(jnp.float32) for j in range(count)]
-        for i in range(count):
-            total = None
-            for j in range(count):
-                if i != j:
-                    term = (coefficient((i - j) % count) * sign) * x[j]
-                    total = term if total is None else total + term
-            mixed_ref[i, panel] = (total * frequency).astype(jnp.bfloat16)
-
-
-def last_kernel(image_ref, sum_ref, mixed_ref, tangent_ref, adjoint_ref):
-    for out_ref, part_ref, panel in ((tangent_ref, image_ref, 0), (adjoint_ref, sum_ref, 1)):
-        out_ref[...] = (part_ref[...] + mixed_ref[:, panel].astype(jnp.float32)).astype(jnp.bfloat16)
+def mix_kernel(frequency_ref, pair_ref, behind_ref, ahead_ref, across_ref, after_ref, keep_ref, send_ref):
+    half, at = place()
+    upper = half == 1
+    scale = jnp.where(upper, -frequency_ref[0], frequency_ref[0])
+
+    def factors(distance, wrapped):
+        same, other = coefficient(distance % INST), coefficient((distance + HALF) % INST)
+        return jnp.where(wrapped, other, same) * scale, jnp.where(wrapped, same, other) * scale
+
+    across, across_other = factors(-2, at >= 2)
+    terms = [
+        (behind_ref, factors(1, at == 0)),
+        (ahead_ref, factors(-1, at == HALF - 1)),
+    ]
+    own = coefficient(HALF) * scale
+    for c in range(pair_ref.shape[1]):
+        first, second = pair_ref[0, c].astype(jnp.float32), pair_ref[1, c].astype(jnp.float32)
+        difference = across_ref[c].astype(jnp.float32)
+        a = own * second + across * difference
+        b = own * first + across_other * difference
+        for ref, (same, other) in terms:
+            first, second = ref[0, c].astype(jnp.float32), ref[1, c].astype(jnp.float32)
+            a = a + same * first + other * second
+            b = b + other * first + same * second
+        keep_ref[c] = jnp.where(upper, b, a)
+        send_ref[c] = jnp.where(upper, a, b).astype(jnp.bfloat16)
+
+
+def last_kernel(image_ref, sum_ref, keep_ref, partner_ref, tangent_ref, adjoint_ref):
+    upper = place()[0] == 1
+    for c in range(image_ref.shape[0]):
+        keep, other = keep_ref[c], partner_ref[c].astype(jnp.float32)
+        tangent_ref[0, c] = (image_ref[c] + jnp.where(upper, other, keep)).astype(jnp.bfloat16)
+        adjoint_ref[0, c] = (sum_ref[c] + jnp.where(upper, keep, other)).astype(jnp.bfloat16)
 
 
 def call(kernel, out, inputs, specs, scratch=(), flops=0, bytes_accessed=0):
@@ -235,7 +246,7 @@
         out_specs=jax.tree.map(lambda _: VMEM, out),
         scratch_shapes=list(scratch),
         cost_estimate=pl.CostEstimate(flops=flops, bytes_accessed=bytes_accessed, transcendentals=0),
-        compiler_params=pltpu.CompilerParams(vmem_limit_bytes=40 << 20),
+        compiler_params=pltpu.CompilerParams(vmem_limit_bytes=52 << 20),
     )(*inputs)
 
 
@@ -245,7 +256,6 @@
     sides = lax.axis_size("inst") // INST
     mesh_size = lax.axis_size("mesh")
     slabs = sides * mesh_size
-    groups = [[side + sides * i for i in range(INST)] for side in range(sides)]
 
     def device(instance, slab):
         return (instance * sides + slab // mesh_size) * mesh_size + slab % mesh_size
@@ -263,31 +273,32 @@
         first = lax.ppermute(first, ("inst", "mesh"), pairs(0))
         return first, second
 
-    def swapped(chunks):
-        return lax.all_to_all(chunks, "inst", 0, 0, axis_index_groups=groups, tiled=True)
+    def moved(value, target):
+        return lax.ppermute(value, "inst", [(i * sides + side, target(i) * sides + side) for i in range(INST) for side in range(sides)])
+
+    def partner(i):
+        return (i + HALF) % INST
+
+    def along(step):
+        return lambda i: i // HALF * HALF + (i + step) % HALF
 
     f32, b16 = jnp.float32, jnp.bfloat16
     shape = jax.ShapeDtypeStruct
-    chunk = shape((INST, 2, columns * block // INST, rows), b16)
     edge = shape((2 * block, rows), b16)
     panel = shape((columns, block, rows), f32)
     loaded = pltpu.VMEM((slots, block, block, rows), b16)
     dma = pltpu.SemaphoreType.DMA
-    copy_of = lambda array: pltpu.VMEM(array.shape, array.dtype)
-    split = lambda array: array.reshape((INST, columns * block // INST, rows))
-    chunks = call(pack_kernel, chunk, (split(tangent_in), split(adjoint_in)), [HBM] * 2, [dma((2,))], bytes_accessed=1 << 19)
-    chunks = swapped(chunks)
+    half = call(half_kernel, shape((8, 128), jnp.int32), (), [], flops=1 << 34)
+    partner_in = moved(jnp.where(half[0, 0] == 0, adjoint_in, tangent_in), partner)
     small = (adjoint_in, tangent_in, neighbors, send_low, send_high)
     own, first, second = call(
         adjoint_kernel,
         (panel, edge, edge),
         (jacobian, *small),
-        [HBM] * 6,
+        [ANY] + [VMEM] * 5,
         [
             loaded,
             dma((slots,)),
-            *map(copy_of, small),
-            dma((len(small),)),
             pltpu.VMEM((columns, block, rows), f32),
             pltpu.VMEM((columns, block, (slots - 1) * rows), b16),
             pltpu.VMEM((columns, block, (slots - 1) * rows), b16),
@@ -295,29 +306,40 @@
         flops=1 << 32,
         bytes_accessed=6 << 20,
     )
+    panels = shape((2, columns, block, rows), b16)
+    one = shape((columns, block, rows), b16)
+    pair, difference = call(
+        pair_kernel, (panels, one), (tangent_in, adjoint_in, partner_in, own), [VMEM] * 3 + [ANY], bytes_accessed=1 << 19
+    )
+    across = moved(difference, along(2))
+    behind = moved(pair, along(1))
+    ahead = moved(pair, along(-1))
     first, second = exchanged(first, second)
-    mixed = call(mix_kernel, chunk, (frequency, chunks, own), [SMEM, VMEM, ANY], bytes_accessed=1 << 19)
-    back = swapped(mixed)
     small = small[1:]
     image, total = call(
         tangent_kernel,
         (panel, panel),
-        (jacobian, *small, first, second, own, mixed),
-        [HBM] * 5 + [VMEM] * 3 + [ANY],
+        (jacobian, *small, first, second, own, pair),
+        [ANY] + [VMEM] * 7 + [ANY],
         [
             loaded,
             dma((4,)),
-            *map(copy_of, small),
-            dma((len(small),)),
             pltpu.VMEM((columns, slots * block, rows), f32),
             pltpu.VMEM((columns * block * 8, rows), f32),
         ],
         flops=1 << 32,
         bytes_accessed=6 << 20,
     )
-    out = shape((INST, columns * block // INST, rows), b16)
-    tangent_out, adjoint_out = call(last_kernel, (out, out), (split(image), split(total), back), [VMEM] * 3, bytes_accessed=1 << 19)
-    return tangent_out.reshape(tangent_in.shape), adjoint_out.reshape(tangent_in.shape)
+    keep, send = call(
+        mix_kernel,
+        (panel, one),
+        (frequency, pair, behind, ahead, across, image),
+        [SMEM] + [VMEM] * 4 + [ANY],
+        bytes_accessed=1 << 19,
+    )
+    other = moved(send, partner)
+    out = shape(tangent_in.shape, b16)
+    return call(last_kernel, (out, out), (image, total, keep, other), [VMEM] * 4, bytes_accessed=1 << 19)
 
 
 def solution(mesh):

time: 50.3 us -> 37.6 us (0.75)
  local copies, waits for them, and re-layouts: 10.4 us -> 0.53 us
  starting transfers between devices: 23.7 us -> 18.9 us
  waiting for transfers between devices: 2.25 us -> 4.05 us
  between operations: 1.4 us -> 2.09 us
    all_to_all x2 -> x0, starting transfers between devices: 16 us -> none  [swapped(): lax.all_to_all(chunks, 'inst', 0, 0, axis_index_groups=groups, tiled=True)]
    ppermute x0 -> x5, starting transfers between devices: none -> 12.1 us  [moved(): lax.ppermute(value, 'inst', [(i * sides + side, target(i) * sides + side)...]
    unnamed x26 -> x10, local copies, waits for them, and re-layouts: 10.4 us -> 0.02 us
    ppermute x0 -> x5, waiting for transfers between devices: none -> 4.05 us  [moved(): lax.ppermute(value, 'inst', [(i * sides + side, target(i) * sides + side)...]
    all_to_all x2 -> x0, waiting for transfers between devices: 2.24 us -> none  [swapped(): lax.all_to_all(chunks, 'inst', 0, 0, axis_index_groups=groups, tiled=True)]
    ppermute x1, starting transfers between devices: 7.62 us -> 6.72 us  [exchanged(): second = lax.ppermute(second, ('inst', 'mesh'), pairs(1))]
    slice x0 -> x1, local copies, waits for them, and re-layouts: none -> 0.51 us  [body(): half[0, 0] == 0]
    pallas_call x5 -> x6, Pallas kernels: 12 us -> 11.8 us  [call(): pl.pallas_call(kernel, out_shape=out, in_specs=specs, out_specs=jax.tree....]
  transfers between devices with their start and end apart: 4 -> 7, of which waited for: 1 -> 1; matrix products, arithmetic and copies ran while one was open for 0% -> 0% of each run, Pallas kernels for 21% -> 29%
where the time goes in v2:
time: 37.6 us; the launch traced here: 37.4 us
  starting transfers between devices  18.9 us (50%)
  Pallas kernels  11.8 us (31%)
  waiting for transfers between devices  4.05 us (11%)
  between operations  2.09 us (6%)
  local copies, waits for them, and re-layouts  0.53 us (1%)
    ppermute x5, starting transfers between devices, moved(): lax.ppermute(value, 'inst', [(i * sides + side, target(i) * sides + side)...  12.1 us
    pallas_call x6, Pallas kernels, call(): pl.pallas_call(kernel, out_shape=out, in_specs=specs, out_specs=jax.tree....  11.8 us
    ppermute x1, starting transfers between devices, exchanged(): second = lax.ppermute(second, ('inst', 'mesh'), pairs(1))  6.72 us
    ppermute x5, waiting for transfers between devices, moved(): lax.ppermute(value, 'inst', [(i * sides + side, target(i) * sides + side)...  4.05 us
  transfers between devices with their start and end apart: 7, of which 1 were waited for; matrix products, arithmetic and copies ran while one was open for 0% of the time, Pallas kernels for 29%

profile of v2, /device:TPU:32, one launch (start us, length us, event | category | flops | bytes accessed | tf_op | source)
XLA Modules:
  0.0 37.4 jit_solution(7727333345051297534)
XLA Ops:
  0.6 0.0 copy-start.1
  0.6 0.0 copy-start
  0.7 0.0 copy-start.4
  0.7 0.0 copy-start.3
  0.7 0.0 copy-start.2
  0.7 0.5 %slice.3 = s32[1,1]{1,0:T(1,128)} slice(s32[8,128]{1,0:T(8,128)S(1)} %shard_map.87), slice={[0:1], [0:1]} | slice | bytes 8 | tf_op jit(solution)/shard_map/slice | solution.py:292
  1.9 0.0 copy-done.1
  1.9 0.0 copy-done
  1.9 1.6 %collective-permute-start.2 = (bf16[1,4,64,128]{3,2,1,0:T(8,128)(2,1)S(1)}, bf16[1,4,64,128]{3,2,1,0:T(8,128)(2,1)S(1)}, u32[]{:S(2)}, u32[]{:S(2)}) collective-permute-start(bf16[1,4,64,128]{3,2,1,0:T(8,128)(2,1)S(1)} %broadcast_select_fusion), channel_id=1, source_target_pairs={{0,128},{16,144},{32,160},{48,176},{64,192},{80,208},{96,224},{112... | collective-permute-start | bytes 196616 | tf_op jit(solution)/shard_map/ppermute | solution.py:277
  3.5 0.0 copy-done.4
  3.5 0.0 copy-done.3
  3.5 0.0 copy-done.2
  3.5 5.7 %shard_map.86 = (f32[4,64,128]{2,1,0:T(8,128)S(1)}, bf16[128,128]{1,0:T(8,128)(2,1)S(1)}, bf16[128,128]{1,0:T(8,128)(2,1)S(1)}) custom-call(bf16[1,5,64,64,128]{4,3,2,1,0:T(8,128)(2,1)} %jac_hbm.3, bf16[1,4,64,128]{3,2,1,0:T(8,128)(2,1)S(1)} %copy-done, bf16[1,4,64,128]{3,2,1,0:T(8,128)(2,1)S(1)} %copy-done.1, s32[2,4,128]{2,1,0:T(4,128)S(1)} %copy-done.2, ...), custom_call_target="tpu_custom_call" | custom-call | flops 4294967296 | bytes 6291456 | tf_op jit(solution)/shard_map/pallas_call | solution.py:242
  9.2 0.1 collective-permute-start
  9.3 6.7 %collective-permute-start.1 = (bf16[128,128]{1,0:T(8,128)(2,1)S(1)}, bf16[128,128]{1,0:T(8,128)(2,1)S(1)}, u32[]{:S(2)}, u32[]{:S(2)}) collective-permute-start(bf16[128,128]{1,0:T(8,128)(2,1)S(1)} %get-tuple-element.12), channel_id=1, source_target_pairs={{1,2},{2,1},{3,4},{4,3},{5,6},{6,5},{7,8},{8,7},{9,10},{10,9},{11,... | collective-permute-start | bytes 98312 | tf_op jit(solution)/shard_map/ppermute | solution.py:272
  16.7 0.0 collective-permute-done.2.partner_ref
  16.7 0.1 shard_map.88
  16.7 6.4 %collective-permute-start.4 = (bf16[2,4,64,128]{3,2,1,0:T(8,128)(2,1)S(1)}, bf16[2,4,64,128]{3,2,1,0:T(8,128)(2,1)S(1)}, u32[]{:S(2)}, u32[]{:S(2)}) collective-permute-start(bf16[2,4,64,128]{3,2,1,0:T(8,128)(2,1)S(1)} %get-tuple-element.14.mixed_ref.pair_ref), channel_id=1, source_target_pairs={{0,96},{16,112},{32,0},{48,16},{64,32},{80,48},{96,64},{112,80},{1... | collective-permute-start | bytes 393224 | tf_op jit(solution)/shard_map/ppermute | solution.py:277
  23.1 0.0 collective-permute-start.3
  23.1 3.8 %collective-permute-start.5 = (bf16[4,64,128]{2,1,0:T(8,128)(2,1)S(1)}, bf16[4,64,128]{2,1,0:T(8,128)(2,1)S(1)}, u32[]{:S(2)}, u32[]{:S(2)}) collective-permute-start(bf16[4,64,128]{2,1,0:T(8,128)(2,1)S(1)} %get-tuple-element.17), channel_id=1, source_target_pairs={{0,64},{16,80},{32,96},{48,112},{64,0},{80,16},{96,32},{112,48},{1... | collective-permute-start | bytes 196616 | tf_op jit(solution)/shard_map/ppermute | solution.py:277
  26.9 0.0 collective-permute-done.first_ref
  26.9 0.0 collective-permute-done.1.second_ref
  26.9 5.2 %shard_map.89 = (f32[4,64,128]{2,1,0:T(8,128)S(1)}, f32[4,64,128]{2,1,0:T(8,128)S(1)}) custom-call(bf16[1,5,64,64,128]{4,3,2,1,0:T(8,128)(2,1)} %jac_hbm.3, bf16[1,4,64,128]{3,2,1,0:T(8,128)(2,1)S(1)} %copy-done.1, s32[2,4,128]{2,1,0:T(4,128)S(1)} %copy-done.2, s32[2,32]{1,0:T(2,128)S(1)} %copy-done.3, s32[2,32]{1,0:T(2,128)S(1)} %copy-done.4, ...), custom_call_target="tpu_custom_call" | custom-call | flops 4294967296 | bytes 6291456 | tf_op jit(solution)/shard_map/pallas_call | solution.py:242
  32.2 0.0 collective-permute-done.5.across_ref
  32.2 0.0 collective-permute-done.4.ahead_ref
  32.2 0.0 collective-permute-done.3.behind_ref
  32.2 0.2 shard_map.90
  32.4 0.3 collective-permute-start.6
  32.7 4.0 %collective-permute-done.6.partner_ref = bf16[4,64,128]{2,1,0:T(8,128)(2,1)S(1)} collective-permute-done((bf16[4,64,128]{2,1,0:T(8,128)(2,1)S(1)}, bf16[4,64,128]{2,1,0:T(8,128)(2,1)S(1)}, u32[]{:S(2)}, u32[]{:S(2)}) %collective-permute-start.6) | collective-permute-done | bytes 65568 | tf_op jit(solution)/shard_map/ppermute | solution.py:277
  36.7 0.7 %shard_map.91 = (bf16[1,4,64,128]{3,2,1,0:T(8,128)(2,1)}, bf16[1,4,64,128]{3,2,1,0:T(8,128)(2,1)}) custom-call(f32[4,64,128]{2,1,0:T(8,128)S(1)} %get-tuple-element.15.after_ref.image_ref, f32[4,64,128]{2,1,0:T(8,128)S(1)} %get-tuple-element.16.sum_ref, f32[4,64,128]{2,1,0:T(8,128)S(1)} %get-tuple-element.18.keep_ref, ...), custom_call_target="tpu_custom_call" | custom-call | bytes 524288 | tf_op jit(solution)/shard_map/pallas_call | solution.py:242
  (2 shorter events, 0.0 us)
Async XLA Ops:
  0.6 1.2 %copy-start.1 = (bf16[1,4,64,128]{3,2,1,0:T(8,128)(2,1)S(1)}, bf16[1,4,64,128]{3,2,1,0:T(8,128)(2,1)}, u32[]{:S(2)}) copy-start(bf16[1,4,64,128]{3,2,1,0:T(8,128)(2,1)} %tangent_ref.5) | copy-start | bytes 196612
  0.6 1.2 %copy-start = (bf16[1,4,64,128]{3,2,1,0:T(8,128)(2,1)S(1)}, bf16[1,4,64,128]{3,2,1,0:T(8,128)(2,1)}, u32[]{:S(2)}) copy-start(bf16[1,4,64,128]{3,2,1,0:T(8,128)(2,1)} %adjoint_ref.3) | copy-start | bytes 196612
  0.7 2.8 %copy-start.4 = (s32[2,32]{1,0:T(2,128)S(1)}, s32[2,32]{1,0:T(2,128)}, u32[]{:S(2)}) copy-start(s32[2,32]{1,0:T(2,128)} %high_ref.3) | copy-start | bytes 772
  0.7 2.8 %copy-start.3 = (s32[2,32]{1,0:T(2,128)S(1)}, s32[2,32]{1,0:T(2,128)}, u32[]{:S(2)}) copy-start(s32[2,32]{1,0:T(2,128)} %low_ref.3) | copy-start | bytes 772
  0.7 2.8 %copy-start.2 = (s32[2,4,128]{2,1,0:T(4,128)S(1)}, s32[2,4,128]{2,1,0:T(4,128)}, u32[]{:S(2)}) copy-start(s32[2,4,128]{2,1,0:T(4,128)} %near_ref.3) | copy-start | bytes 12292
  1.9 14.7 %collective-permute-start.2 = (bf16[1,4,64,128]{3,2,1,0:T(8,128)(2,1)S(1)}, bf16[1,4,64,128]{3,2,1,0:T(8,128)(2,1)S(1)}, u32[]{:S(2)}, u32[]{:S(2)}) collective-permute-start(bf16[1,4,64,128]{3,2,1,0:T(8,128)(2,1)S(1)} %broadcast_select_fusion), channel_id=1, source_target_pairs={{0,128},{16,144},{32,160},{48,176},{64,192},{80,208},{96,224},{112... | collective-permute-start | bytes 196616 | tf_op jit(solution)/shard_map/ppermute | solution.py:277
  9.2 17.8 %collective-permute-start = (bf16[128,128]{1,0:T(8,128)(2,1)S(1)}, bf16[128,128]{1,0:T(8,128)(2,1)S(1)}, u32[]{:S(2)}, u32[]{:S(2)}) collective-permute-start(bf16[128,128]{1,0:T(8,128)(2,1)S(1)} %get-tuple-element.11), channel_id=1, source_target_pairs={{0,1},{1,0},{2,3},{3,2},{4,5},{5,4},{6,7},{7,6},{8,9},{9,8},{10,11... | collective-permute-start | bytes 98312 | tf_op jit(solution)/shard_map/ppermute | solution.py:273
  9.3 17.7 %collective-permute-start.1 = (bf16[128,128]{1,0:T(8,128)(2,1)S(1)}, bf16[128,128]{1,0:T(8,128)(2,1)S(1)}, u32[]{:S(2)}, u32[]{:S(2)}) collective-permute-start(bf16[128,128]{1,0:T(8,128)(2,1)S(1)} %get-tuple-element.12), channel_id=1, source_target_pairs={{1,2},{2,1},{3,4},{4,3},{5,6},{6,5},{7,8},{8,7},{9,10},{10,9},{11,... | collective-permute-start | bytes 98312 | tf_op jit(solution)/shard_map/ppermute | solution.py:272
  16.7 15.4 %collective-permute-start.4 = (bf16[2,4,64,128]{3,2,1,0:T(8,128)(2,1)S(1)}, bf16[2,4,64,128]{3,2,1,0:T(8,128)(2,1)S(1)}, u32[]{:S(2)}, u32[]{:S(2)}) collective-permute-start(bf16[2,4,64,128]{3,2,1,0:T(8,128)(2,1)S(1)} %get-tuple-element.14.mixed_ref.pair_ref), channel_id=1, source_target_pairs={{0,96},{16,112},{32,0},{48,16},{64,32},{80,48},{96,64},{112,80},{1... | collective-permute-start | bytes 393224 | tf_op jit(solution)/shard_map/ppermute | solution.py:277
  23.1 9.1 %collective-permute-start.3 = (bf16[2,4,64,128]{3,2,1,0:T(8,128)(2,1)S(1)}, bf16[2,4,64,128]{3,2,1,0:T(8,128)(2,1)S(1)}, u32[]{:S(2)}, u32[]{:S(2)}) collective-permute-start(bf16[2,4,64,128]{3,2,1,0:T(8,128)(2,1)S(1)} %get-tuple-element.14.mixed_ref.pair_ref), channel_id=1, source_target_pairs={{0,32},{16,48},{32,64},{48,80},{64,96},{80,112},{96,0},{112,16},{1... | collective-permute-start | bytes 393224 | tf_op jit(solution)/shard_map/ppermute | solution.py:277
  23.1 9.1 %collective-permute-start.5 = (bf16[4,64,128]{2,1,0:T(8,128)(2,1)S(1)}, bf16[4,64,128]{2,1,0:T(8,128)(2,1)S(1)}, u32[]{:S(2)}, u32[]{:S(2)}) collective-permute-start(bf16[4,64,128]{2,1,0:T(8,128)(2,1)S(1)} %get-tuple-element.17), channel_id=1, source_target_pairs={{0,64},{16,80},{32,96},{48,112},{64,0},{80,16},{96,32},{112,48},{1... | collective-permute-start | bytes 196616 | tf_op jit(solution)/shard_map/ppermute | solution.py:277
  32.4 4.4 %collective-permute-start.6 = (bf16[4,64,128]{2,1,0:T(8,128)(2,1)S(1)}, bf16[4,64,128]{2,1,0:T(8,128)(2,1)S(1)}, u32[]{:S(2)}, u32[]{:S(2)}) collective-permute-start(bf16[4,64,128]{2,1,0:T(8,128)(2,1)S(1)} %get-tuple-element.19), channel_id=1, source_target_pairs={{0,128},{16,144},{32,160},{48,176},{64,192},{80,208},{96,224},{112... | collective-permute-start | bytes 196616 | tf_op jit(solution)/shard_map/ppermute | solution.py:277

commit v3 on v2

--- a/solution.py
+++ b/solution.py
@@ -10,7 +10,6 @@
 INST = 8
 HALF = INST // 2
 VMEM = pl.BlockSpec(memory_space=pltpu.VMEM)
-SMEM = pl.BlockSpec(memory_space=pltpu.SMEM)
 ANY = pl.BlockSpec(memory_space=pl.ANY)
 
 
@@ -58,13 +57,6 @@
     return (at == wide).astype(jnp.float32).astype(jnp.bfloat16)
 
 
-def copied(pairs, sem):
-    copies = [pltpu.make_async_copy(source, target, sem.at[i]) for i, (source, target) in enumerate(pairs)]
-    for copy in copies:
-        copy.start()
-    return copies
-
-
 def half_kernel(half_ref):
     half_ref[...] = jnp.full(half_ref.shape, place()[0], jnp.int32)
 
@@ -78,59 +70,65 @@
     difference_ref[...] = (first.astype(jnp.float32) - second.astype(jnp.float32)).astype(jnp.bfloat16)
 
 
-def adjoint_kernel(
-    jac_hbm, adjoint_ref, tangent_ref, near_ref, low_ref, high_ref, own_ref, first_ref, second_ref,
-    jac_ref, sem, weights, high, low
+def slot_products(jac_ref, weights, slot):
+    columns, block, rows = weights.shape
+
+    def step(a, acc):
+        jac = jac_ref[0, slot, a].astype(jnp.float32)
+        return tuple(acc[c] + jac * weights[c, pl.ds(a, 1), :] for c in range(columns))
+
+    zero = tuple(jnp.zeros((block, rows), jnp.float32) for _ in range(columns))
+    return lax.fori_loop(0, block, step, zero, unroll=16)
+
+
+def neighbor_products(jac_ref, adjoint_ref, high, low, weights, start, stop):
+    columns, _, rows = weights.shape
+    for c in range(columns):
+        weights[c] = adjoint_ref[0, c].astype(jnp.float32)
+
+    def one_slot(k, carry):
+        acc = slot_products(jac_ref, weights, k)
+        at = pl.ds(pl.multiple_of((k - start) * rows, rows), rows)
+        for c in range(columns):
+            top = acc[c].astype(jnp.bfloat16)
+            high[c, :, at] = top
+            low[c, :, at] = (acc[c] - top.astype(jnp.float32)).astype(jnp.bfloat16)
+        return carry
+
+    lax.fori_loop(start, stop, one_slot, 0)
+
+
+def adjoint_kernel(jac_ref, adjoint_ref, high_ref, low_ref, weights):
+    count = high_ref.shape[2] // weights.shape[2]
+    neighbor_products(jac_ref, adjoint_ref, high_ref, low_ref, weights, 1, 1 + count)
+
+
+def return_kernel(
+    jac_ref, adjoint_ref, tangent_ref, near_ref, send_low_ref, send_high_ref, high_ref, low_ref, after_ref, after_too_ref,
+    own_ref, first_ref, second_ref, weights, high, low
 ):
-    columns, block, rows = adjoint_ref.shape[1:]
-    slots = jac_ref.shape[0]
+    columns, block, rows = weights.shape
     halo = rows // columns
-    copies = copied([(jac_hbm.at[0, k], jac_ref.at[k]) for k in range(slots)], sem)
-    rows_out = send_matrix(low_ref, high_ref, columns, rows)
+    done = high_ref.shape[2] // rows
+    rows_out = send_matrix(send_low_ref, send_high_ref, columns, rows)
     wide = jnp.concatenate([tangent_ref[0, c] for c in range(columns)], axis=1)
     out = jnp.dot(wide, rows_out, preferred_element_type=jnp.float32).astype(jnp.bfloat16)
     first_ref[:block] = out[:, :rows]
     second_ref[:block] = out[:, rows:]
-    for c in range(columns):
-        weights[c] = adjoint_ref[0, c].astype(jnp.float32)
-
-    def one_slot(k, keep):
-        def step(a, acc):
-            jac = jac_ref[k, a].astype(jnp.float32)
-            return tuple(acc[c] + jac * weights[c, pl.ds(a, 1), :] for c in range(columns))
-
-        zero = tuple(jnp.zeros((block, rows), jnp.float32) for _ in range(columns))
-        acc = lax.fori_loop(0, block, step, zero, unroll=8)
-        for c in range(columns):
-            keep(c, acc[c])
-
-    def keep_own(c, value):
-        own_ref[c] = value
-
-    copies[0].wait()
-    one_slot(0, keep_own)
-
-    def other_slot(k, carry):
-        def keep(c, value):
-            top = value.astype(jnp.bfloat16)
-            at = pl.ds(pl.multiple_of((k - 1) * rows, rows), rows)
-            high[c, :, at] = top
-            low[c, :, at] = (value - top.astype(jnp.float32)).astype(jnp.bfloat16)
-
-        pltpu.make_async_copy(jac_hbm.at[0, k], jac_ref.at[k], sem.at[k]).wait()
-        one_slot(k, keep)
-        return carry
-
-    lax.fori_loop(1, slots, other_slot, 0)
+    neighbor_products(jac_ref, adjoint_ref, high, low, weights, 1 + done, jac_ref.shape[1])
+    own = slot_products(jac_ref, weights, 0)
     matrix = neighbor_matrix(near_ref, rows, halo)
+    before, after = matrix[:, : done * rows], matrix[:, done * rows :]
     transposed = (((1,), (1,)), ((), ()))
     lane = lax.broadcasted_iota(jnp.int32, (block, rows), 1)
     first = jnp.zeros((block, rows), jnp.float32)
     second = jnp.zeros((block, rows), jnp.float32)
     for c in range(columns):
-        q = lax.dot_general(high[c], matrix, transposed, preferred_element_type=jnp.float32)
-        q = q + lax.dot_general(low[c], matrix, transposed, preferred_element_type=jnp.float32)
-        own_ref[c] = own_ref[c] + q[:, :rows]
+        q = sum(
+            lax.dot_general(ref[c], part, transposed, preferred_element_type=jnp.float32)
+            for ref, part in ((high_ref, before), (low_ref, before), (high, after), (low, after))
+        )
+        own_ref[c] = own[c] + q[:, :rows]
         edge = q[:, rows:]
         here = lane // halo == c
         first = jnp.where(here, pltpu.roll(edge, (halo * c) % rows, 1), first)
@@ -140,18 +138,13 @@
 
 
 def tangent_kernel(
-    jac_hbm, tangent_ref, near_ref, low_ref, high_ref, first_ref, second_ref, own_ref, mixed_ref, image_ref, sum_ref,
-    jac_ref, sem, picked, partial
+    jac_ref, tangent_ref, near_ref, low_ref, high_ref, first_ref, second_ref, own_ref, after_ref, image_ref, sum_ref, picked, partial
 ):
     columns, block, rows = tangent_ref.shape[1:]
-    slots = jac_ref.shape[0]
+    slots = jac_ref.shape[1]
     halo = rows // columns
-    group = 4
+    group = 8
     deep = 16
-    loads = sem.shape[0]
-    load = block // loads
-    parts = [pl.ds(part * load, load) for part in range(loads)]
-    copies = copied([(jac_hbm.at[0, :, at], jac_ref.at[:, at]) for at in parts], sem)
     matrix = neighbor_matrix(near_ref, rows, halo)
     lane = lax.broadcasted_iota(jnp.int32, (block, rows), 1)
     first = first_ref[:block].astype(jnp.float32)
@@ -168,44 +161,41 @@
         for k in range(slots - 1):
             picked[c, (k + 1) * block : (k + 2) * block] = wide[:, k * rows : (k + 1) * rows]
 
+    back = jnp.concatenate([first_ref[block:], second_ref[block:]], axis=1)
+    out = send_matrix(low_ref, high_ref, columns, rows)
+    added = lax.dot_general(back, out, (((1,), (1,)), ((), ())), preferred_element_type=jnp.float32)
+    for c in range(columns):
+        sum_ref[c] = own_ref[c] + added[:, c * rows : (c + 1) * rows]
+
     def one_group(g, carry):
         acc = [[jnp.zeros((8, rows), jnp.float32) for _ in range(columns)] for _ in range(group)]
         for k in range(slots):
             for b in range(0, block, deep):
                 x = [picked[c, k * block + b : k * block + b + deep] for c in range(columns)]
                 for a in range(group):
-                    jac = jac_ref[k, g * group + a, b : b + deep, :].astype(jnp.float32)
+                    jac = jac_ref[0, k, g * group + a, b : b + deep, :].astype(jnp.float32)
                     for c in range(columns):
                         product = jac * x[c]
-                        acc[a][c] = acc[a][c] + product[:8] + product[8:]
-        for a in range(group):
-            for c in range(columns):
-                at = pl.multiple_of((c * block + g * group + a) * 8, 8)
-                partial[pl.ds(at, 8), :] = acc[a][c]
+                        acc[a][c] = acc[a][c] + (product[:8] + product[8:])
+        for c in range(columns):
+            for a in range(group):
+                partial[c, a * 8 : (a + 1) * 8] = acc[a][c]
+        at = pl.ds(pl.multiple_of(g * group, group), group)
+        for c in range(columns):
+            total = partial[c, pl.ds(0, 8, stride=8), :]
+            for s in range(1, 8):
+                total = total + partial[c, pl.ds(s, 8, stride=8), :]
+            image_ref[c, at] = total
         return carry
 
-    per = load // group
-    for part in range(loads):
-        copies[part].wait()
-        lax.fori_loop(part * per, (part + 1) * per, one_group, 0)
-    for c in range(columns):
-        for a in range(0, block, 8):
-            base = (c * block + a) * 8
-            total = partial[pl.ds(base, 8, stride=8), :]
-            for s in range(1, 8):
-                total = total + partial[pl.ds(base + s, 8, stride=8), :]
-            image_ref[c, a : a + 8] = total
-    back = jnp.concatenate([first_ref[block:], second_ref[block:]], axis=1)
-    out = send_matrix(low_ref, high_ref, columns, rows)
-    added = lax.dot_general(back, out, (((1,), (1,)), ((), ())), preferred_element_type=jnp.float32)
-    for c in range(columns):
-        sum_ref[c] = own_ref[c] + added[:, c * rows : (c + 1) * rows]
+    lax.fori_loop(0, block // group, one_group, 0)
 
 
 def mix_kernel(frequency_ref, pair_ref, behind_ref, ahead_ref, across_ref, after_ref, keep_ref, send_ref):
     half, at = place()
     upper = half == 1
-    scale = jnp.where(upper, -frequency_ref[0], frequency_ref[0])
+    frequency = frequency_ref[...]
+    scale = jnp.where(upper, -frequency, frequency)
 
     def factors(distance, wrapped):
         same, other = coefficient(distance % INST), coefficient((distance + HALF) % INST)
@@ -246,7 +236,7 @@
         out_specs=jax.tree.map(lambda _: VMEM, out),
         scratch_shapes=list(scratch),
         cost_estimate=pl.CostEstimate(flops=flops, bytes_accessed=bytes_accessed, transcendentals=0),
-        compiler_params=pltpu.CompilerParams(vmem_limit_bytes=52 << 20),
+        compiler_params=pltpu.CompilerParams(vmem_limit_bytes=44 << 20),
     )(*inputs)
 
 
@@ -286,58 +276,55 @@
     shape = jax.ShapeDtypeStruct
     edge = shape((2 * block, rows), b16)
     panel = shape((columns, block, rows), f32)
-    loaded = pltpu.VMEM((slots, block, block, rows), b16)
-    dma = pltpu.SemaphoreType.DMA
-    half = call(half_kernel, shape((8, 128), jnp.int32), (), [], flops=1 << 34)
-    partner_in = moved(jnp.where(half[0, 0] == 0, adjoint_in, tangent_in), partner)
-    small = (adjoint_in, tangent_in, neighbors, send_low, send_high)
-    own, first, second = call(
+    half = call(half_kernel, shape((1, rows), jnp.int32), (), [], flops=1 << 34)
+    partner_in = moved(jnp.where(half.reshape((1, 1, 1, rows)) == 0, adjoint_in, tangent_in), partner)
+    weights = pltpu.VMEM((columns, block, rows), f32)
+    done = (slots + 1) // 2
+    later = slots - 1 - done
+    high, low = call(
         adjoint_kernel,
-        (panel, edge, edge),
-        (jacobian, *small),
-        [ANY] + [VMEM] * 5,
-        [
-            loaded,
-            dma((slots,)),
-            pltpu.VMEM((columns, block, rows), f32),
-            pltpu.VMEM((columns, block, (slots - 1) * rows), b16),
-            pltpu.VMEM((columns, block, (slots - 1) * rows), b16),
-        ],
-        flops=1 << 32,
+        (shape((columns, block, done * rows), b16),) * 2,
+        (jacobian, adjoint_in),
+        [VMEM] * 2,
+        [weights],
+        flops=1 << 31,
         bytes_accessed=6 << 20,
     )
     panels = shape((2, columns, block, rows), b16)
     one = shape((columns, block, rows), b16)
     pair, difference = call(
-        pair_kernel, (panels, one), (tangent_in, adjoint_in, partner_in, own), [VMEM] * 3 + [ANY], bytes_accessed=1 << 19
+        pair_kernel, (panels, one), (tangent_in, adjoint_in, partner_in, high), [VMEM] * 3 + [ANY], bytes_accessed=1 << 19
     )
     across = moved(difference, along(2))
     behind = moved(pair, along(1))
     ahead = moved(pair, along(-1))
+    own, first, second = call(
+        return_kernel,
+        (panel, edge, edge),
+        (jacobian, adjoint_in, tangent_in, neighbors, send_low, send_high, high, low, pair, difference),
+        [VMEM] * 8 + [ANY] * 2,
+        [weights] + [pltpu.VMEM((columns, block, later * rows), b16)] * 2,
+        flops=1 << 31,
+        bytes_accessed=6 << 20,
+    )
     first, second = exchanged(first, second)
-    small = small[1:]
+    keep, send = call(
+        mix_kernel,
+        (panel, one),
+        (frequency.reshape((1, 1)), pair, behind, ahead, across, own),
+        [VMEM] * 5 + [ANY],
+        bytes_accessed=1 << 19,
+    )
+    other = moved(send, partner)
     image, total = call(
         tangent_kernel,
         (panel, panel),
-        (jacobian, *small, first, second, own, pair),
-        [ANY] + [VMEM] * 7 + [ANY],
-        [
-            loaded,
-            dma((4,)),
-            pltpu.VMEM((columns, slots * block, rows), f32),
-            pltpu.VMEM((columns * block * 8, rows), f32),
-        ],
+        (jacobian, tangent_in, neighbors, send_low, send_high, first, second, own, keep),
+        [VMEM] * 8 + [ANY],
+        [pltpu.VMEM((columns, slots * block, rows), f32), pltpu.VMEM((columns, 64, rows), f32)],
         flops=1 << 32,
         bytes_accessed=6 << 20,
     )
-    keep, send = call(
-        mix_kernel,
-        (panel, one),
-        (frequency, pair, behind, ahead, across, image),
-        [SMEM] + [VMEM] * 4 + [ANY],
-        bytes_accessed=1 << 19,
-    )
-    other = moved(send, partner)
     out = shape(tangent_in.shape, b16)
     return call(last_kernel, (out, out), (image, total, keep, other), [VMEM] * 4, bytes_accessed=1 << 19)
 

time: 37.6 us -> 33.6 us (0.89)
  the two profiles are of different devices: /device:TPU:32 before, /device:TPU:29 now
where the time goes in v3:
time: 33.6 us; the launch traced here: 33.5 us
  starting transfers between devices  16.6 us (49%)
  Pallas kernels  9.19 us (27%)
  waiting for transfers between devices  4.77 us (14%)
  local copies, waits for them, and re-layouts  1.46 us (4%)
  between operations  1.43 us (4%)
    ppermute x5, starting transfers between devices, moved(): lax.ppermute(value, 'inst', [(i * sides + side, target(i) * sides + side)...  12.3 us
    pallas_call x7, Pallas kernels, call(): pl.pallas_call(kernel, out_shape=out, in_specs=specs, out_specs=jax.tree....  9.19 us
    ppermute x1, waiting for transfers between devices, exchanged(): second = lax.ppermute(second, ('inst', 'mesh'), pairs(1))  4.75 us
    ppermute x1, starting transfers between devices, exchanged(): first = lax.ppermute(first, ('inst', 'mesh'), pairs(0))  2.23 us
    ppermute x1, starting transfers between devices, exchanged(): second = lax.ppermute(second, ('inst', 'mesh'), pairs(1))  2.14 us
    unnamed x12, local copies, waits for them, and re-layouts  1.46 us
  transfers between devices with their start and end apart: 7, of which 1 were waited for; matrix products, arithmetic and copies ran while one was open for 0% of the time, Pallas kernels for 25%

profile of v3, /device:TPU:29, one launch (start us, length us, event | category | flops | bytes accessed | tf_op | source)
XLA Modules:
  0.0 33.5 jit_solution(16473066496511293702)
XLA Ops:
  0.6 0.0 copy-start
  0.6 0.0 copy-start.1
  0.6 0.0 copy-start.2
  0.7 0.0 copy-start.3
  0.7 0.0 copy-start.4
  0.7 0.0 copy-start.5
  0.7 0.7 %copy-done = bf16[1,4,64,128]{3,2,1,0:T(8,128)(2,1)S(1)} copy-done((bf16[1,4,64,128]{3,2,1,0:T(8,128)(2,1)S(1)}, bf16[1,4,64,128]{3,2,1,0:T(8,128)(2,1)}, u32[]{:S(2)}) %copy-start) | copy-done | bytes 65560
  1.5 0.0 copy-done.1
  1.5 1.0 %collective-permute-start = (bf16[1,4,64,128]{3,2,1,0:T(8,128)(2,1)S(1)}, bf16[1,4,64,128]{3,2,1,0:T(8,128)(2,1)S(1)}, u32[]{:S(2)}, u32[]{:S(2)}) collective-permute-start(bf16[1,4,64,128]{3,2,1,0:T(8,128)(2,1)S(1)} %broadcast_select_fusion), channel_id=1, source_target_pairs={{0,128},{16,144},{32,160},{48,176},{64,192},{80,208},{96,224},{112... | collective-permute-start | bytes 196616 | tf_op jit(solution)/shard_map/ppermute | solution.py:267
  2.5 0.7 %copy-done.2 = bf16[1,5,64,64,128]{4,3,2,1,0:T(8,128)(2,1)S(1)} copy-done((bf16[1,5,64,64,128]{4,3,2,1,0:T(8,128)(2,1)S(1)}, bf16[1,5,64,64,128]{4,3,2,1,0:T(8,128)(2,1)}, u32[]{:S(2)}) %copy-start.2) | copy-done | bytes 5242904
  3.2 2.0 %shard_map.86 = (bf16[4,64,384]{2,1,0:T(8,128)(2,1)S(1)}, bf16[4,64,384]{2,1,0:T(8,128)(2,1)S(1)}) custom-call(bf16[1,5,64,64,128]{4,3,2,1,0:T(8,128)(2,1)S(1)} %copy-done.2, bf16[1,4,64,128]{3,2,1,0:T(8,128)(2,1)S(1)} %copy-done), custom_call_target="tpu_custom_call" | custom-call | flops 2147483648 | bytes 6291456 | tf_op jit(solution)/shard_map/pallas_call | solution.py:232
  5.2 0.0 collective-permute-done.partner_ref
  5.2 0.1 shard_map.88
  5.3 6.1 %collective-permute-start.4 = (bf16[2,4,64,128]{3,2,1,0:T(8,128)(2,1)S(1)}, bf16[2,4,64,128]{3,2,1,0:T(8,128)(2,1)S(1)}, u32[]{:S(2)}, u32[]{:S(2)}) collective-permute-start(bf16[2,4,64,128]{3,2,1,0:T(8,128)(2,1)S(1)} %get-tuple-element.15.after_ref.pair_ref), channel_id=1, source_target_pairs={{0,96},{16,112},{32,0},{48,16},{64,32},{80,48},{96,64},{112,80},{1... | collective-permute-start | bytes 393224 | tf_op jit(solution)/shard_map/ppermute | solution.py:267
  11.4 0.0 collective-permute-start.3
  11.4 3.3 %collective-permute-start.5 = (bf16[4,64,128]{2,1,0:T(8,128)(2,1)S(1)}, bf16[4,64,128]{2,1,0:T(8,128)(2,1)S(1)}, u32[]{:S(2)}, u32[]{:S(2)}) collective-permute-start(bf16[4,64,128]{2,1,0:T(8,128)(2,1)S(1)} %get-tuple-element.16.after_too_ref), channel_id=1, source_target_pairs={{0,64},{16,80},{32,96},{48,112},{64,0},{80,16},{96,32},{112,48},{1... | collective-permute-start | bytes 196616 | tf_op jit(solution)/shard_map/ppermute | solution.py:267
  14.7 0.0 copy-done.3
  14.7 0.0 copy-done.4
  14.7 0.0 copy-done.5
  14.7 2.4 %shard_map.89 = (f32[4,64,128]{2,1,0:T(8,128)S(1)}, bf16[128,128]{1,0:T(8,128)(2,1)S(1)}, bf16[128,128]{1,0:T(8,128)(2,1)S(1)}) custom-call(bf16[1,5,64,64,128]{4,3,2,1,0:T(8,128)(2,1)S(1)} %copy-done.2, bf16[1,4,64,128]{3,2,1,0:T(8,128)(2,1)S(1)} %copy-done, bf16[1,4,64,128]{3,2,1,0:T(8,128)(2,1)S(1)} %copy-done.1, s32[2,4,128]{2,1,0:T(4,128)S(1)} %copy-done.3, ...), custom_call_target="tpu_custom_call" | custom-call | flops 2147483648 | bytes 6291456 | tf_op jit(solution)/shard_map/pallas_call | solution.py:232
  17.1 2.2 %collective-permute-start.1 = (bf16[128,128]{1,0:T(8,128)(2,1)S(1)}, bf16[128,128]{1,0:T(8,128)(2,1)S(1)}, u32[]{:S(2)}, u32[]{:S(2)}) collective-permute-start(bf16[128,128]{1,0:T(8,128)(2,1)S(1)} %get-tuple-element.17), channel_id=1, source_target_pairs={{0,1},{1,0},{2,3},{3,2},{4,5},{5,4},{6,7},{7,6},{8,9},{9,8},{10,11... | collective-permute-start | bytes 98312 | tf_op jit(solution)/shard_map/ppermute | solution.py:263
  19.3 2.1 %collective-permute-start.2 = (bf16[128,128]{1,0:T(8,128)(2,1)S(1)}, bf16[128,128]{1,0:T(8,128)(2,1)S(1)}, u32[]{:S(2)}, u32[]{:S(2)}) collective-permute-start(bf16[128,128]{1,0:T(8,128)(2,1)S(1)} %get-tuple-element.18), channel_id=1, source_target_pairs={{1,2},{2,1},{3,4},{4,3},{5,6},{6,5},{7,8},{8,7},{9,10},{10,9},{11,... | collective-permute-start | bytes 98312 | tf_op jit(solution)/shard_map/ppermute | solution.py:262
  22.1 0.0 collective-permute-done.5.across_ref
  22.2 0.0 collective-permute-done.4.ahead_ref
  22.2 0.0 collective-permute-done.3.behind_ref
  22.2 0.2 shard_map.90
  22.4 1.9 %collective-permute-start.6 = (bf16[4,64,128]{2,1,0:T(8,128)(2,1)S(1)}, bf16[4,64,128]{2,1,0:T(8,128)(2,1)S(1)}, u32[]{:S(2)}, u32[]{:S(2)}) collective-permute-start(bf16[4,64,128]{2,1,0:T(8,128)(2,1)S(1)} %get-tuple-element.23), channel_id=1, source_target_pairs={{0,128},{16,144},{32,160},{48,176},{64,192},{80,208},{96,224},{112... | collective-permute-start | bytes 196616 | tf_op jit(solution)/shard_map/ppermute | solution.py:267
  24.3 0.0 collective-permute-done.1.first_ref
  24.3 4.8 %collective-permute-done.2.second_ref = bf16[128,128]{1,0:T(8,128)(2,1)S(1)} collective-permute-done((bf16[128,128]{1,0:T(8,128)(2,1)S(1)}, bf16[128,128]{1,0:T(8,128)(2,1)S(1)}, u32[]{:S(2)}, u32[]{:S(2)}) %collective-permute-start.2) | collective-permute-done | bytes 32800 | tf_op jit(solution)/shard_map/ppermute | solution.py:262
  29.1 3.7 %shard_map.91 = (f32[4,64,128]{2,1,0:T(8,128)S(1)}, f32[4,64,128]{2,1,0:T(8,128)S(1)}) custom-call(bf16[1,5,64,64,128]{4,3,2,1,0:T(8,128)(2,1)S(1)} %copy-done.2, bf16[1,4,64,128]{3,2,1,0:T(8,128)(2,1)S(1)} %copy-done.1, s32[2,4,128]{2,1,0:T(4,128)S(1)} %copy-done.3, s32[2,32]{1,0:T(2,128)S(1)} %copy-done.4, s32[2,32]{1,0:T(2,128)S(1)} %copy-done.5, ...), custom_call_target="tpu_custom_call" | custom-call | flops 4294967296 | bytes 6291456 | tf_op jit(solution)/shard_map/pallas_call | solution.py:232
  32.8 0.0 collective-permute-done.6.partner_ref
  32.8 0.7 %shard_map.92 = (bf16[1,4,64,128]{3,2,1,0:T(8,128)(2,1)}, bf16[1,4,64,128]{3,2,1,0:T(8,128)(2,1)}) custom-call(f32[4,64,128]{2,1,0:T(8,128)S(1)} %get-tuple-element.21.image_ref, f32[4,64,128]{2,1,0:T(8,128)S(1)} %get-tuple-element.22.sum_ref, f32[4,64,128]{2,1,0:T(8,128)S(1)} %get-tuple-element.20.after_ref.keep_ref, ...), custom_call_target="tpu_custom_call" | custom-call | bytes 524288 | tf_op jit(solution)/shard_map/pallas_call | solution.py:232
  (3 shorter events, 0.0 us)
Async XLA Ops:
  0.6 0.8 %copy-start = (bf16[1,4,64,128]{3,2,1,0:T(8,128)(2,1)S(1)}, bf16[1,4,64,128]{3,2,1,0:T(8,128)(2,1)}, u32[]{:S(2)}) copy-start(bf16[1,4,64,128]{3,2,1,0:T(8,128)(2,1)} %adjoint_ref.5) | copy-start | bytes 196612
  0.6 0.9 %copy-start.1 = (bf16[1,4,64,128]{3,2,1,0:T(8,128)(2,1)S(1)}, bf16[1,4,64,128]{3,2,1,0:T(8,128)(2,1)}, u32[]{:S(2)}) copy-start(bf16[1,4,64,128]{3,2,1,0:T(8,128)(2,1)} %tangent_ref.5) | copy-start | bytes 196612
  0.6 2.5 %copy-start.2 = (bf16[1,5,64,64,128]{4,3,2,1,0:T(8,128)(2,1)S(1)}, bf16[1,5,64,64,128]{4,3,2,1,0:T(8,128)(2,1)}, u32[]{:S(2)}) copy-start(bf16[1,5,64,64,128]{4,3,2,1,0:T(8,128)(2,1)} %jac_ref.5) | copy-start | bytes 15728644
  0.7 14.0 %copy-start.3 = (s32[2,4,128]{2,1,0:T(4,128)S(1)}, s32[2,4,128]{2,1,0:T(4,128)}, u32[]{:S(2)}) copy-start(s32[2,4,128]{2,1,0:T(4,128)} %near_ref.3) | copy-start | bytes 12292
  0.7 14.0 %copy-start.4 = (s32[2,32]{1,0:T(2,128)S(1)}, s32[2,32]{1,0:T(2,128)}, u32[]{:S(2)}) copy-start(s32[2,32]{1,0:T(2,128)} %low_ref.1) | copy-start | bytes 772
  0.7 14.0 %copy-start.5 = (s32[2,32]{1,0:T(2,128)S(1)}, s32[2,32]{1,0:T(2,128)}, u32[]{:S(2)}) copy-start(s32[2,32]{1,0:T(2,128)} %high_ref.1) | copy-start | bytes 772
  1.5 3.7 %collective-permute-start = (bf16[1,4,64,128]{3,2,1,0:T(8,128)(2,1)S(1)}, bf16[1,4,64,128]{3,2,1,0:T(8,128)(2,1)S(1)}, u32[]{:S(2)}, u32[]{:S(2)}) collective-permute-start(bf16[1,4,64,128]{3,2,1,0:T(8,128)(2,1)S(1)} %broadcast_select_fusion), channel_id=1, source_target_pairs={{0,128},{16,144},{32,160},{48,176},{64,192},{80,208},{96,224},{112... | collective-permute-start | bytes 196616 | tf_op jit(solution)/shard_map/ppermute | solution.py:267
  5.3 16.8 %collective-permute-start.4 = (bf16[2,4,64,128]{3,2,1,0:T(8,128)(2,1)S(1)}, bf16[2,4,64,128]{3,2,1,0:T(8,128)(2,1)S(1)}, u32[]{:S(2)}, u32[]{:S(2)}) collective-permute-start(bf16[2,4,64,128]{3,2,1,0:T(8,128)(2,1)S(1)} %get-tuple-element.15.after_ref.pair_ref), channel_id=1, source_target_pairs={{0,96},{16,112},{32,0},{48,16},{64,32},{80,48},{96,64},{112,80},{1... | collective-permute-start | bytes 393224 | tf_op jit(solution)/shard_map/ppermute | solution.py:267
  11.4 10.8 %collective-permute-start.3 = (bf16[2,4,64,128]{3,2,1,0:T(8,128)(2,1)S(1)}, bf16[2,4,64,128]{3,2,1,0:T(8,128)(2,1)S(1)}, u32[]{:S(2)}, u32[]{:S(2)}) collective-permute-start(bf16[2,4,64,128]{3,2,1,0:T(8,128)(2,1)S(1)} %get-tuple-element.15.after_ref.pair_ref), channel_id=1, source_target_pairs={{0,32},{16,48},{32,64},{48,80},{64,96},{80,112},{96,0},{112,16},{1... | collective-permute-start | bytes 393224 | tf_op jit(solution)/shard_map/ppermute | solution.py:267
  11.4 10.7 %collective-permute-start.5 = (bf16[4,64,128]{2,1,0:T(8,128)(2,1)S(1)}, bf16[4,64,128]{2,1,0:T(8,128)(2,1)S(1)}, u32[]{:S(2)}, u32[]{:S(2)}) collective-permute-start(bf16[4,64,128]{2,1,0:T(8,128)(2,1)S(1)} %get-tuple-element.16.after_too_ref), channel_id=1, source_target_pairs={{0,64},{16,80},{32,96},{48,112},{64,0},{80,16},{96,32},{112,48},{1... | collective-permute-start | bytes 196616 | tf_op jit(solution)/shard_map/ppermute | solution.py:267
  17.1 7.2 %collective-permute-start.1 = (bf16[128,128]{1,0:T(8,128)(2,1)S(1)}, bf16[128,128]{1,0:T(8,128)(2,1)S(1)}, u32[]{:S(2)}, u32[]{:S(2)}) collective-permute-start(bf16[128,128]{1,0:T(8,128)(2,1)S(1)} %get-tuple-element.17), channel_id=1, source_target_pairs={{0,1},{1,0},{2,3},{3,2},{4,5},{5,4},{6,7},{7,6},{8,9},{9,8},{10,11... | collective-permute-start | bytes 98312 | tf_op jit(solution)/shard_map/ppermute | solution.py:263
  19.3 9.7 %collective-permute-start.2 = (bf16[128,128]{1,0:T(8,128)(2,1)S(1)}, bf16[128,128]{1,0:T(8,128)(2,1)S(1)}, u32[]{:S(2)}, u32[]{:S(2)}) collective-permute-start(bf16[128,128]{1,0:T(8,128)(2,1)S(1)} %get-tuple-element.18), channel_id=1, source_target_pairs={{1,2},{2,1},{3,4},{4,3},{5,6},{6,5},{7,8},{8,7},{9,10},{10,9},{11,... | collective-permute-start | bytes 98312 | tf_op jit(solution)/shard_map/ppermute | solution.py:262
  22.4 10.4 %collective-permute-start.6 = (bf16[4,64,128]{2,1,0:T(8,128)(2,1)S(1)}, bf16[4,64,128]{2,1,0:T(8,128)(2,1)S(1)}, u32[]{:S(2)}, u32[]{:S(2)}) collective-permute-start(bf16[4,64,128]{2,1,0:T(8,128)(2,1)S(1)} %get-tuple-element.23), channel_id=1, source_target_pairs={{0,128},{16,144},{32,160},{48,176},{64,192},{80,208},{96,224},{112... | collective-permute-start | bytes 196616 | tf_op jit(solution)/shard_map/ppermute | solution.py:267

commit v4 on v3

--- a/solution.py
+++ b/solution.py
@@ -28,6 +28,12 @@
     return lax.axis_index("inst") % sides, lax.axis_index("mesh") % 2
 
 
+def at_end():
+    side, _ = side_and_odd()
+    slab = side * lax.axis_size("mesh") + lax.axis_index("mesh")
+    return (slab == 0) | (slab == lax.axis_size("inst") // INST * lax.axis_size("mesh") - 1)
+
+
 def picked_side(ref, side):
     return jnp.where(side == 0, ref[0], ref[1])
 
@@ -38,6 +44,7 @@
     high = jnp.where(side == 0, high_ref[0:1], high_ref[1:2])
     first = jnp.where(odd == 1, low, high)
     second = jnp.where(odd == 1, high, low)
+    second = jnp.where(at_end(), -columns * rows, second)
     places = [part + rows * c for part in (first, second) for c in range(columns)]
     target = jnp.concatenate(places, axis=1)
     at = lax.broadcasted_iota(jnp.int32, (columns * rows, target.shape[1]), 0)
@@ -50,6 +57,7 @@
     swapped = jnp.where(near >= rows + halo, near - halo, near + halo)
     inside = near < rows
     outside = jnp.where(odd == 1, near, swapped)
+    outside = jnp.where(at_end() & (outside >= rows + halo), -1, outside)
     index = jnp.where(inside, near, jnp.where(near >= rows + 2 * halo, -1, outside))
     slots = near.shape[0]
     wide = jnp.concatenate([index[k : k + 1] for k in range(slots)], axis=1)
@@ -98,9 +106,13 @@
     lax.fori_loop(start, stop, one_slot, 0)
 
 
-def adjoint_kernel(jac_ref, adjoint_ref, high_ref, low_ref, weights):
+def adjoint_kernel(jac_ref, adjoint_ref, frequency_hbm, high_ref, low_ref, frequency_ref, weights, scalar, sem):
+    copy = pltpu.make_async_copy(frequency_hbm, scalar, sem)
+    copy.start()
     count = high_ref.shape[2] // weights.shape[2]
     neighbor_products(jac_ref, adjoint_ref, high_ref, low_ref, weights, 1, 1 + count)
+    copy.wait()
+    frequency_ref[...] = jnp.full(frequency_ref.shape, scalar[0])
 
 
 def return_kernel(
@@ -256,6 +268,9 @@
             for slab in range(start, slabs - 1, 2):
                 low, high = device(instance, slab), device(instance, slab + 1)
                 found += [(low, high), (high, low)]
+            if start == 1:
+                low, high = device(instance, 0), device(instance, slabs - 1)
+                found += [(low, high), (high, low)]
         return found
 
     def exchanged(first, second):
@@ -281,12 +296,13 @@
     weights = pltpu.VMEM((columns, block, rows), f32)
     done = (slots + 1) // 2
     later = slots - 1 - done
-    high, low = call(
+    half_terms = shape((columns, block, done * rows), b16)
+    high, low, frequency = call(
         adjoint_kernel,
-        (shape((columns, block, done * rows), b16),) * 2,
-        (jacobian, adjoint_in),
-        [VMEM] * 2,
-        [weights],
+        (half_terms, half_terms, shape((1, rows), f32)),
+        (jacobian, adjoint_in, frequency),
+        [VMEM] * 2 + [ANY],
+        [weights, pltpu.SMEM((1,), f32), pltpu.SemaphoreType.DMA],
         flops=1 << 31,
         bytes_accessed=6 << 20,
     )
@@ -311,7 +327,7 @@
     keep, send = call(
         mix_kernel,
         (panel, one),
-        (frequency.reshape((1, 1)), pair, behind, ahead, across, own),
+        (frequency, pair, behind, ahead, across, own),
         [VMEM] * 5 + [ANY],
         bytes_accessed=1 << 19,
     )

time: 33.6 us -> 31.7 us (0.943)
  starting transfers between devices: 16.6 us -> 14.8 us
  waiting for transfers between devices: 4.77 us -> 5.43 us
  local copies, waits for them, and re-layouts: 1.46 us -> 0.81 us
    ppermute x1, starting transfers between devices: 2.14 us -> 0.32 us  [exchanged(): second = lax.ppermute(second, ('inst', 'mesh'), pairs(1))]
    ppermute x1, waiting for transfers between devices: 4.75 us -> 5.42 us  [exchanged(): second = lax.ppermute(second, ('inst', 'mesh'), pairs(1))]
    unnamed x12, local copies, waits for them, and re-layouts: 1.46 us -> 0.81 us
  transfers between devices with their start and end apart: 7 -> 7, of which waited for: 1 -> 1; matrix products, arithmetic and copies ran while one was open for 0% -> 0% of each run, Pallas kernels for 25% -> 26%
where the time goes in v4:
time: 31.7 us; the launch traced here: 31.6 us
  starting transfers between devices  14.8 us (47%)
  Pallas kernels  9.14 us (29%)
  waiting for transfers between devices  5.43 us (17%)
  between operations  1.41 us (4%)
  local copies, waits for them, and re-layouts  0.81 us (3%)
    ppermute x5, starting transfers between devices, moved(): lax.ppermute(value, 'inst', [(i * sides + side, target(i) * sides + side)...  12.3 us
    pallas_call x7, Pallas kernels, call(): pl.pallas_call(kernel, out_shape=out, in_specs=specs, out_specs=jax.tree....  9.14 us
    ppermute x1, waiting for transfers between devices, exchanged(): second = lax.ppermute(second, ('inst', 'mesh'), pairs(1))  5.42 us
    ppermute x1, starting transfers between devices, exchanged(): first = lax.ppermute(first, ('inst', 'mesh'), pairs(0))  2.21 us
    unnamed x12, local copies, waits for them, and re-layouts  0.81 us
  transfers between devices with their start and end apart: 7, of which 1 were waited for; matrix products, arithmetic and copies ran while one was open for 0% of the time, Pallas kernels for 26%

profile of v4, /device:TPU:29, one launch (start us, length us, event | category | flops | bytes accessed | tf_op | source)
XLA Modules:
  0.0 31.6 jit_solution(17419438805769270014)
XLA Ops:
  0.6 0.0 copy-start
  0.6 0.0 copy-start.1
  0.6 0.0 copy-start.2
  0.7 0.0 copy-start.3
  0.7 0.0 copy-start.4
  0.7 0.0 copy-start.5
  0.7 0.7 %copy-done = bf16[1,4,64,128]{3,2,1,0:T(8,128)(2,1)S(1)} copy-done((bf16[1,4,64,128]{3,2,1,0:T(8,128)(2,1)S(1)}, bf16[1,4,64,128]{3,2,1,0:T(8,128)(2,1)}, u32[]{:S(2)}) %copy-start) | copy-done | bytes 65560
  1.5 0.0 copy-done.1
  1.5 1.0 %collective-permute-start = (bf16[1,4,64,128]{3,2,1,0:T(8,128)(2,1)S(1)}, bf16[1,4,64,128]{3,2,1,0:T(8,128)(2,1)S(1)}, u32[]{:S(2)}, u32[]{:S(2)}) collective-permute-start(bf16[1,4,64,128]{3,2,1,0:T(8,128)(2,1)S(1)} %broadcast_select_fusion), channel_id=1, source_target_pairs={{0,128},{16,144},{32,160},{48,176},{64,192},{80,208},{96,224},{112... | collective-permute-start | bytes 196616 | tf_op jit(solution)/shard_map/ppermute | solution.py:282
  3.2 0.0 copy-done.2
  3.2 2.0 %shard_map.86 = (bf16[4,64,384]{2,1,0:T(8,128)(2,1)S(1)}, bf16[4,64,384]{2,1,0:T(8,128)(2,1)S(1)}, f32[1,128]{1,0:T(1,128)S(1)}) custom-call(bf16[1,5,64,64,128]{4,3,2,1,0:T(8,128)(2,1)S(1)} %copy-done.2, bf16[1,4,64,128]{3,2,1,0:T(8,128)(2,1)S(1)} %copy-done, f32[1]{0:T(128)S(6)} %copy.9.frequency_hbm), custom_call_target="tpu_custom_call" | custom-call | flops 2147483648 | bytes 6291456 | tf_op jit(solution)/shard_map/pallas_call | solution.py:244
  5.2 0.0 collective-permute-done.partner_ref
  5.3 0.1 shard_map.88
  5.3 6.1 %collective-permute-start.4 = (bf16[2,4,64,128]{3,2,1,0:T(8,128)(2,1)S(1)}, bf16[2,4,64,128]{3,2,1,0:T(8,128)(2,1)S(1)}, u32[]{:S(2)}, u32[]{:S(2)}) collective-permute-start(bf16[2,4,64,128]{3,2,1,0:T(8,128)(2,1)S(1)} %get-tuple-element.16.after_ref.pair_ref), channel_id=1, source_target_pairs={{0,96},{16,112},{32,0},{48,16},{64,32},{80,48},{96,64},{112,80},{1... | collective-permute-start | bytes 393224 | tf_op jit(solution)/shard_map/ppermute | solution.py:282
  11.4 0.0 collective-permute-start.3
  11.4 3.3 %collective-permute-start.5 = (bf16[4,64,128]{2,1,0:T(8,128)(2,1)S(1)}, bf16[4,64,128]{2,1,0:T(8,128)(2,1)S(1)}, u32[]{:S(2)}, u32[]{:S(2)}) collective-permute-start(bf16[4,64,128]{2,1,0:T(8,128)(2,1)S(1)} %get-tuple-element.17.after_too_ref), channel_id=1, source_target_pairs={{0,64},{16,80},{32,96},{48,112},{64,0},{80,16},{96,32},{112,48},{1... | collective-permute-start | bytes 196616 | tf_op jit(solution)/shard_map/ppermute | solution.py:282
  14.7 0.0 copy-done.3
  14.7 0.0 copy-done.4
  14.7 0.0 copy-done.5
  14.7 2.4 %shard_map.89 = (f32[4,64,128]{2,1,0:T(8,128)S(1)}, bf16[128,128]{1,0:T(8,128)(2,1)S(1)}, bf16[128,128]{1,0:T(8,128)(2,1)S(1)}) custom-call(bf16[1,5,64,64,128]{4,3,2,1,0:T(8,128)(2,1)S(1)} %copy-done.2, bf16[1,4,64,128]{3,2,1,0:T(8,128)(2,1)S(1)} %copy-done, bf16[1,4,64,128]{3,2,1,0:T(8,128)(2,1)S(1)} %copy-done.1, s32[2,4,128]{2,1,0:T(4,128)S(1)} %copy-done.3, ...), custom_call_target="tpu_custom_call" | custom-call | flops 2147483648 | bytes 6291456 | tf_op jit(solution)/shard_map/pallas_call | solution.py:244
  17.1 2.2 %collective-permute-start.1 = (bf16[128,128]{1,0:T(8,128)(2,1)S(1)}, bf16[128,128]{1,0:T(8,128)(2,1)S(1)}, u32[]{:S(2)}, u32[]{:S(2)}) collective-permute-start(bf16[128,128]{1,0:T(8,128)(2,1)S(1)} %get-tuple-element.18), channel_id=1, source_target_pairs={{0,1},{1,0},{2,3},{3,2},{4,5},{5,4},{6,7},{7,6},{8,9},{9,8},{10,11... | collective-permute-start | bytes 98312 | tf_op jit(solution)/shard_map/ppermute | solution.py:278
  19.3 0.3 %collective-permute-start.2 = (bf16[128,128]{1,0:T(8,128)(2,1)S(1)}, bf16[128,128]{1,0:T(8,128)(2,1)S(1)}, u32[]{:S(2)}, u32[]{:S(2)}) collective-permute-start(bf16[128,128]{1,0:T(8,128)(2,1)S(1)} %get-tuple-element.19), channel_id=1, source_target_pairs={{1,2},{2,1},{3,4},{4,3},{5,6},{6,5},{7,8},{8,7},{9,10},{10,9},{11,... | collective-permute-start | bytes 98312 | tf_op jit(solution)/shard_map/ppermute | solution.py:277
  19.7 0.0 collective-permute-done.5.across_ref
  19.7 0.0 collective-permute-done.4.ahead_ref
  19.7 0.0 collective-permute-done.3.behind_ref
  19.7 0.2 shard_map.90
  19.9 1.9 %collective-permute-start.6 = (bf16[4,64,128]{2,1,0:T(8,128)(2,1)S(1)}, bf16[4,64,128]{2,1,0:T(8,128)(2,1)S(1)}, u32[]{:S(2)}, u32[]{:S(2)}) collective-permute-start(bf16[4,64,128]{2,1,0:T(8,128)(2,1)S(1)} %get-tuple-element.25), channel_id=1, source_target_pairs={{0,128},{16,144},{32,160},{48,176},{64,192},{80,208},{96,224},{112... | collective-permute-start | bytes 196616 | tf_op jit(solution)/shard_map/ppermute | solution.py:282
  21.8 0.0 collective-permute-done.1.first_ref
  21.8 5.4 %collective-permute-done.2.second_ref = bf16[128,128]{1,0:T(8,128)(2,1)S(1)} collective-permute-done((bf16[128,128]{1,0:T(8,128)(2,1)S(1)}, bf16[128,128]{1,0:T(8,128)(2,1)S(1)}, u32[]{:S(2)}, u32[]{:S(2)}) %collective-permute-start.2) | collective-permute-done | bytes 32800 | tf_op jit(solution)/shard_map/ppermute | solution.py:277
  27.2 3.7 %shard_map.91 = (f32[4,64,128]{2,1,0:T(8,128)S(1)}, f32[4,64,128]{2,1,0:T(8,128)S(1)}) custom-call(bf16[1,5,64,64,128]{4,3,2,1,0:T(8,128)(2,1)S(1)} %copy-done.2, bf16[1,4,64,128]{3,2,1,0:T(8,128)(2,1)S(1)} %copy-done.1, s32[2,4,128]{2,1,0:T(4,128)S(1)} %copy-done.3, s32[2,32]{1,0:T(2,128)S(1)} %copy-done.4, s32[2,32]{1,0:T(2,128)S(1)} %copy-done.5, ...), custom_call_target="tpu_custom_call" | custom-call | flops 4294967296 | bytes 6291456 | tf_op jit(solution)/shard_map/pallas_call | solution.py:244
  30.9 0.0 collective-permute-done.6.partner_ref
  30.9 0.7 %shard_map.92 = (bf16[1,4,64,128]{3,2,1,0:T(8,128)(2,1)}, bf16[1,4,64,128]{3,2,1,0:T(8,128)(2,1)}) custom-call(f32[4,64,128]{2,1,0:T(8,128)S(1)} %get-tuple-element.23.image_ref, f32[4,64,128]{2,1,0:T(8,128)S(1)} %get-tuple-element.24.sum_ref, f32[4,64,128]{2,1,0:T(8,128)S(1)} %get-tuple-element.22.after_ref.keep_ref, ...), custom_call_target="tpu_custom_call" | custom-call | bytes 524288 | tf_op jit(solution)/shard_map/pallas_call | solution.py:244
  (3 shorter events, 0.0 us)
Async XLA Ops:
  0.6 0.8 %copy-start = (bf16[1,4,64,128]{3,2,1,0:T(8,128)(2,1)S(1)}, bf16[1,4,64,128]{3,2,1,0:T(8,128)(2,1)}, u32[]{:S(2)}) copy-start(bf16[1,4,64,128]{3,2,1,0:T(8,128)(2,1)} %adjoint_ref.5) | copy-start | bytes 196612
  0.6 0.9 %copy-start.1 = (bf16[1,4,64,128]{3,2,1,0:T(8,128)(2,1)S(1)}, bf16[1,4,64,128]{3,2,1,0:T(8,128)(2,1)}, u32[]{:S(2)}) copy-start(bf16[1,4,64,128]{3,2,1,0:T(8,128)(2,1)} %tangent_ref.5) | copy-start | bytes 196612
  0.6 2.5 %copy-start.2 = (bf16[1,5,64,64,128]{4,3,2,1,0:T(8,128)(2,1)S(1)}, bf16[1,5,64,64,128]{4,3,2,1,0:T(8,128)(2,1)}, u32[]{:S(2)}) copy-start(bf16[1,5,64,64,128]{4,3,2,1,0:T(8,128)(2,1)} %jac_ref.5) | copy-start | bytes 15728644
  0.7 14.0 %copy-start.3 = (s32[2,4,128]{2,1,0:T(4,128)S(1)}, s32[2,4,128]{2,1,0:T(4,128)}, u32[]{:S(2)}) copy-start(s32[2,4,128]{2,1,0:T(4,128)} %near_ref.3) | copy-start | bytes 12292
  0.7 14.0 %copy-start.4 = (s32[2,32]{1,0:T(2,128)S(1)}, s32[2,32]{1,0:T(2,128)}, u32[]{:S(2)}) copy-start(s32[2,32]{1,0:T(2,128)} %low_ref.1) | copy-start | bytes 772
  0.7 14.0 %copy-start.5 = (s32[2,32]{1,0:T(2,128)S(1)}, s32[2,32]{1,0:T(2,128)}, u32[]{:S(2)}) copy-start(s32[2,32]{1,0:T(2,128)} %high_ref.1) | copy-start | bytes 772
  1.5 3.7 %collective-permute-start = (bf16[1,4,64,128]{3,2,1,0:T(8,128)(2,1)S(1)}, bf16[1,4,64,128]{3,2,1,0:T(8,128)(2,1)S(1)}, u32[]{:S(2)}, u32[]{:S(2)}) collective-permute-start(bf16[1,4,64,128]{3,2,1,0:T(8,128)(2,1)S(1)} %broadcast_select_fusion), channel_id=1, source_target_pairs={{0,128},{16,144},{32,160},{48,176},{64,192},{80,208},{96,224},{112... | collective-permute-start | bytes 196616 | tf_op jit(solution)/shard_map/ppermute | solution.py:282
  5.3 14.3 %collective-permute-start.4 = (bf16[2,4,64,128]{3,2,1,0:T(8,128)(2,1)S(1)}, bf16[2,4,64,128]{3,2,1,0:T(8,128)(2,1)S(1)}, u32[]{:S(2)}, u32[]{:S(2)}) collective-permute-start(bf16[2,4,64,128]{3,2,1,0:T(8,128)(2,1)S(1)} %get-tuple-element.16.after_ref.pair_ref), channel_id=1, source_target_pairs={{0,96},{16,112},{32,0},{48,16},{64,32},{80,48},{96,64},{112,80},{1... | collective-permute-start | bytes 393224 | tf_op jit(solution)/shard_map/ppermute | solution.py:282
  11.4 8.2 %collective-permute-start.3 = (bf16[2,4,64,128]{3,2,1,0:T(8,128)(2,1)S(1)}, bf16[2,4,64,128]{3,2,1,0:T(8,128)(2,1)S(1)}, u32[]{:S(2)}, u32[]{:S(2)}) collective-permute-start(bf16[2,4,64,128]{3,2,1,0:T(8,128)(2,1)S(1)} %get-tuple-element.16.after_ref.pair_ref), channel_id=1, source_target_pairs={{0,32},{16,48},{32,64},{48,80},{64,96},{80,112},{96,0},{112,16},{1... | collective-permute-start | bytes 393224 | tf_op jit(solution)/shard_map/ppermute | solution.py:282
  11.4 8.2 %collective-permute-start.5 = (bf16[4,64,128]{2,1,0:T(8,128)(2,1)S(1)}, bf16[4,64,128]{2,1,0:T(8,128)(2,1)S(1)}, u32[]{:S(2)}, u32[]{:S(2)}) collective-permute-start(bf16[4,64,128]{2,1,0:T(8,128)(2,1)S(1)} %get-tuple-element.17.after_too_ref), channel_id=1, source_target_pairs={{0,64},{16,80},{32,96},{48,112},{64,0},{80,16},{96,32},{112,48},{1... | collective-permute-start | bytes 196616 | tf_op jit(solution)/shard_map/ppermute | solution.py:282
  17.1 4.6 %collective-permute-start.1 = (bf16[128,128]{1,0:T(8,128)(2,1)S(1)}, bf16[128,128]{1,0:T(8,128)(2,1)S(1)}, u32[]{:S(2)}, u32[]{:S(2)}) collective-permute-start(bf16[128,128]{1,0:T(8,128)(2,1)S(1)} %get-tuple-element.18), channel_id=1, source_target_pairs={{0,1},{1,0},{2,3},{3,2},{4,5},{5,4},{6,7},{7,6},{8,9},{9,8},{10,11... | collective-permute-start | bytes 98312 | tf_op jit(solution)/shard_map/ppermute | solution.py:278
  19.3 7.9 %collective-permute-start.2 = (bf16[128,128]{1,0:T(8,128)(2,1)S(1)}, bf16[128,128]{1,0:T(8,128)(2,1)S(1)}, u32[]{:S(2)}, u32[]{:S(2)}) collective-permute-start(bf16[128,128]{1,0:T(8,128)(2,1)S(1)} %get-tuple-element.19), channel_id=1, source_target_pairs={{1,2},{2,1},{3,4},{4,3},{5,6},{6,5},{7,8},{8,7},{9,10},{10,9},{11,... | collective-permute-start | bytes 98312 | tf_op jit(solution)/shard_map/ppermute | solution.py:277
  19.9 11.0 %collective-permute-start.6 = (bf16[4,64,128]{2,1,0:T(8,128)(2,1)S(1)}, bf16[4,64,128]{2,1,0:T(8,128)(2,1)S(1)}, u32[]{:S(2)}, u32[]{:S(2)}) collective-permute-start(bf16[4,64,128]{2,1,0:T(8,128)(2,1)S(1)} %get-tuple-element.25), channel_id=1, source_target_pairs={{0,128},{16,144},{32,160},{48,176},{64,192},{80,208},{96,224},{112... | collective-permute-start | bytes 196616 | tf_op jit(solution)/shard_map/ppermute | solution.py:282

commit v5 on v4

--- a/solution.py
+++ b/solution.py
@@ -106,31 +106,36 @@
     lax.fori_loop(start, stop, one_slot, 0)
 
 
-def adjoint_kernel(jac_ref, adjoint_ref, frequency_hbm, high_ref, low_ref, frequency_ref, weights, scalar, sem):
+def adjoint_kernel(
+    jac_ref, adjoint_ref, near_ref, send_low_ref, send_high_ref, frequency_hbm, high_ref, low_ref, near_matrix_ref, send_matrix_ref,
+    frequency_ref, weights, scalar, sem
+):
     copy = pltpu.make_async_copy(frequency_hbm, scalar, sem)
     copy.start()
     count = high_ref.shape[2] // weights.shape[2]
     neighbor_products(jac_ref, adjoint_ref, high_ref, low_ref, weights, 1, 1 + count)
+    columns, _, rows = weights.shape
+    near_matrix_ref[...] = neighbor_matrix(near_ref, rows, rows // columns)
+    send_matrix_ref[...] = send_matrix(send_low_ref, send_high_ref, columns, rows)
     copy.wait()
     frequency_ref[...] = jnp.full(frequency_ref.shape, scalar[0])
 
 
 def return_kernel(
-    jac_ref, adjoint_ref, tangent_ref, near_ref, send_low_ref, send_high_ref, high_ref, low_ref, after_ref, after_too_ref,
+    jac_ref, adjoint_ref, tangent_ref, near_matrix_ref, send_matrix_ref, high_ref, low_ref, after_ref, after_too_ref,
     own_ref, first_ref, second_ref, weights, high, low
 ):
     columns, block, rows = weights.shape
     halo = rows // columns
     done = high_ref.shape[2] // rows
-    rows_out = send_matrix(send_low_ref, send_high_ref, columns, rows)
+    rows_out = send_matrix_ref[...]
     wide = jnp.concatenate([tangent_ref[0, c] for c in range(columns)], axis=1)
     out = jnp.dot(wide, rows_out, preferred_element_type=jnp.float32).astype(jnp.bfloat16)
     first_ref[:block] = out[:, :rows]
     second_ref[:block] = out[:, rows:]
     neighbor_products(jac_ref, adjoint_ref, high, low, weights, 1 + done, jac_ref.shape[1])
     own = slot_products(jac_ref, weights, 0)
-    matrix = neighbor_matrix(near_ref, rows, halo)
-    before, after = matrix[:, : done * rows], matrix[:, done * rows :]
+    before, after = near_matrix_ref[:, : done * rows], near_matrix_ref[:, done * rows :]
     transposed = (((1,), (1,)), ((), ()))
     lane = lax.broadcasted_iota(jnp.int32, (block, rows), 1)
     first = jnp.zeros((block, rows), jnp.float32)
@@ -150,14 +155,14 @@
 
 
 def tangent_kernel(
-    jac_ref, tangent_ref, near_ref, low_ref, high_ref, first_ref, second_ref, own_ref, after_ref, image_ref, sum_ref, picked, partial
+    jac_ref, tangent_ref, near_matrix_ref, send_matrix_ref, first_ref, second_ref, own_ref, after_ref, image_ref, sum_ref, picked, partial
 ):
     columns, block, rows = tangent_ref.shape[1:]
     slots = jac_ref.shape[1]
     halo = rows // columns
     group = 8
     deep = 16
-    matrix = neighbor_matrix(near_ref, rows, halo)
+    matrix = near_matrix_ref[...]
     lane = lax.broadcasted_iota(jnp.int32, (block, rows), 1)
     first = first_ref[:block].astype(jnp.float32)
     second = second_ref[:block].astype(jnp.float32)
@@ -174,7 +179,7 @@
             picked[c, (k + 1) * block : (k + 2) * block] = wide[:, k * rows : (k + 1) * rows]
 
     back = jnp.concatenate([first_ref[block:], second_ref[block:]], axis=1)
-    out = send_matrix(low_ref, high_ref, columns, rows)
+    out = send_matrix_ref[...]
     added = lax.dot_general(back, out, (((1,), (1,)), ((), ())), preferred_element_type=jnp.float32)
     for c in range(columns):
         sum_ref[c] = own_ref[c] + added[:, c * rows : (c + 1) * rows]
@@ -269,8 +274,7 @@
                 low, high = device(instance, slab), device(instance, slab + 1)
                 found += [(low, high), (high, low)]
             if start == 1:
-                low, high = device(instance, 0), device(instance, slabs - 1)
-                found += [(low, high), (high, low)]
+                found += [(device(instance, slab), device((instance + HALF) % INST, slab)) for slab in (0, slabs - 1)]
         return found
 
     def exchanged(first, second):
@@ -297,11 +301,12 @@
     done = (slots + 1) // 2
     later = slots - 1 - done
     half_terms = shape((columns, block, done * rows), b16)
-    high, low, frequency = call(
+    matrices = shape((2 * rows, (slots - 1) * rows), b16), shape((columns * rows, 2 * rows), b16)
+    high, low, near_matrix, out_matrix, frequency = call(
         adjoint_kernel,
-        (half_terms, half_terms, shape((1, rows), f32)),
-        (jacobian, adjoint_in, frequency),
-        [VMEM] * 2 + [ANY],
+        (half_terms, half_terms, *matrices, shape((1, rows), f32)),
+        (jacobian, adjoint_in, neighbors, send_low, send_high, frequency),
+        [VMEM] * 5 + [ANY],
         [weights, pltpu.SMEM((1,), f32), pltpu.SemaphoreType.DMA],
         flops=1 << 31,
         bytes_accessed=6 << 20,
@@ -317,8 +322,8 @@
     own, first, second = call(
         return_kernel,
         (panel, edge, edge),
-        (jacobian, adjoint_in, tangent_in, neighbors, send_low, send_high, high, low, pair, difference),
-        [VMEM] * 8 + [ANY] * 2,
+        (jacobian, adjoint_in, tangent_in, near_matrix, out_matrix, high, low, pair, difference),
+        [VMEM] * 7 + [ANY] * 2,
         [weights] + [pltpu.VMEM((columns, block, later * rows), b16)] * 2,
         flops=1 << 31,
         bytes_accessed=6 << 20,
@@ -335,8 +340,8 @@
     image, total = call(
         tangent_kernel,
         (panel, panel),
-        (jacobian, tangent_in, neighbors, send_low, send_high, first, second, own, keep),
-        [VMEM] * 8 + [ANY],
+        (jacobian, tangent_in, near_matrix, out_matrix, first, second, own, keep),
+        [VMEM] * 7 + [ANY],
         [pltpu.VMEM((columns, slots * block, rows), f32), pltpu.VMEM((columns, 64, rows), f32)],
         flops=1 << 32,
         bytes_accessed=6 << 20,

time: 31.7 us -> 31.6 us (level)
  transfers between devices with their start and end apart: 7 -> 7, of which waited for: 1 -> 1; matrix products, arithmetic and copies ran while one was open for 0% -> 0% of each run, Pallas kernels for 26% -> 27%
where the time goes in v5:
time: 31.6 us; the launch traced here: 31.5 us
  starting transfers between devices  14.5 us (46%)
  Pallas kernels  9.27 us (29%)
  waiting for transfers between devices  5.47 us (17%)
  between operations  1.42 us (4%)
  local copies, waits for them, and re-layouts  0.81 us (3%)
    ppermute x5, starting transfers between devices, moved(): lax.ppermute(value, 'inst', [(i * sides + side, target(i) * sides + side)...  12 us
    pallas_call x7, Pallas kernels, call(): pl.pallas_call(kernel, out_shape=out, in_specs=specs, out_specs=jax.tree....  9.27 us
    ppermute x1, waiting for transfers between devices, exchanged(): second = lax.ppermute(second, ('inst', 'mesh'), pairs(1))  5.46 us
    ppermute x1, starting transfers between devices, exchanged(): first = lax.ppermute(first, ('inst', 'mesh'), pairs(0))  1.97 us
    unnamed x12, local copies, waits for them, and re-layouts  0.81 us
  transfers between devices with their start and end apart: 7, of which 1 were waited for; matrix products, arithmetic and copies ran while one was open for 0% of the time, Pallas kernels for 27%

profile of v5, /device:TPU:29, one launch (start us, length us, event | category | flops | bytes accessed | tf_op | source)
XLA Modules:
  0.0 31.5 jit_solution(2720817565102316521)
XLA Ops:
  0.6 0.0 copy-start
  0.6 0.0 copy-start.1
  0.7 0.0 copy-start.2
  0.7 0.0 copy-start.5
  0.7 0.0 copy-start.4
  0.7 0.0 copy-start.3
  0.7 0.7 %copy-done = bf16[1,4,64,128]{3,2,1,0:T(8,128)(2,1)S(1)} copy-done((bf16[1,4,64,128]{3,2,1,0:T(8,128)(2,1)S(1)}, bf16[1,4,64,128]{3,2,1,0:T(8,128)(2,1)}, u32[]{:S(2)}) %copy-start) | copy-done | bytes 65560
  1.5 0.0 copy-done.1
  1.5 1.0 %collective-permute-start = (bf16[1,4,64,128]{3,2,1,0:T(8,128)(2,1)S(1)}, bf16[1,4,64,128]{3,2,1,0:T(8,128)(2,1)S(1)}, u32[]{:S(2)}, u32[]{:S(2)}) collective-permute-start(bf16[1,4,64,128]{3,2,1,0:T(8,128)(2,1)S(1)} %broadcast_select_fusion), channel_id=1, source_target_pairs={{0,128},{16,144},{32,160},{48,176},{64,192},{80,208},{96,224},{112... | collective-permute-start | bytes 196616 | tf_op jit(solution)/shard_map/ppermute | solution.py:286
  3.2 0.0 copy-done.2
  3.2 0.0 copy-done.5
  3.2 0.0 copy-done.4
  3.2 0.0 copy-done.3
  3.2 2.3 %shard_map.86 = (bf16[4,64,384]{2,1,0:T(8,128)(2,1)S(1)}, bf16[4,64,384]{2,1,0:T(8,128)(2,1)S(1)}, bf16[256,512]{1,0:T(8,128)(2,1)S(1)}, bf16[512,256]{1,0:T(8,128)(2,1)S(1)}, f32[1,128]{1,0:T(1,128)S(1)}) custom-call(bf16[1,5,64,64,128]{4,3,2,1,0:T(8,128)(2,1)S(1)} %copy-done.2, bf16[1,4,64,128]{3,2,1,0:T(8,128)(2,1)S(1)} %copy-done, ...), custom_call_target="tpu_custom_call" | custom-call | flops 2147483648 | bytes 6291456 | tf_op jit(solution)/shard_map/pallas_call | solution.py:249
  5.5 0.0 collective-permute-done.partner_ref
  5.5 0.1 shard_map.88
  5.6 6.1 %collective-permute-start.4 = (bf16[2,4,64,128]{3,2,1,0:T(8,128)(2,1)S(1)}, bf16[2,4,64,128]{3,2,1,0:T(8,128)(2,1)S(1)}, u32[]{:S(2)}, u32[]{:S(2)}) collective-permute-start(bf16[2,4,64,128]{3,2,1,0:T(8,128)(2,1)S(1)} %get-tuple-element.20.after_ref.pair_ref), channel_id=1, source_target_pairs={{0,96},{16,112},{32,0},{48,16},{64,32},{80,48},{96,64},{112,80},{1... | collective-permute-start | bytes 393224 | tf_op jit(solution)/shard_map/ppermute | solution.py:286
  11.7 0.0 collective-permute-start.3
  11.7 3.3 %collective-permute-start.5 = (bf16[4,64,128]{2,1,0:T(8,128)(2,1)S(1)}, bf16[4,64,128]{2,1,0:T(8,128)(2,1)S(1)}, u32[]{:S(2)}, u32[]{:S(2)}) collective-permute-start(bf16[4,64,128]{2,1,0:T(8,128)(2,1)S(1)} %get-tuple-element.21.after_too_ref), channel_id=1, source_target_pairs={{0,64},{16,80},{32,96},{48,112},{64,0},{80,16},{96,32},{112,48},{1... | collective-permute-start | bytes 196616 | tf_op jit(solution)/shard_map/ppermute | solution.py:286
  14.9 2.3 %shard_map.89 = (f32[4,64,128]{2,1,0:T(8,128)S(1)}, bf16[128,128]{1,0:T(8,128)(2,1)S(1)}, bf16[128,128]{1,0:T(8,128)(2,1)S(1)}) custom-call(bf16[1,5,64,64,128]{4,3,2,1,0:T(8,128)(2,1)S(1)} %copy-done.2, bf16[1,4,64,128]{3,2,1,0:T(8,128)(2,1)S(1)} %copy-done, bf16[1,4,64,128]{3,2,1,0:T(8,128)(2,1)S(1)} %copy-done.1, ...), custom_call_target="tpu_custom_call" | custom-call | flops 2147483648 | bytes 6291456 | tf_op jit(solution)/shard_map/pallas_call | solution.py:249
  17.3 2.0 %collective-permute-start.1 = (bf16[128,128]{1,0:T(8,128)(2,1)S(1)}, bf16[128,128]{1,0:T(8,128)(2,1)S(1)}, u32[]{:S(2)}, u32[]{:S(2)}) collective-permute-start(bf16[128,128]{1,0:T(8,128)(2,1)S(1)} %get-tuple-element.22), channel_id=1, source_target_pairs={{0,1},{1,0},{2,3},{3,2},{4,5},{5,4},{6,7},{7,6},{8,9},{9,8},{10,11... | collective-permute-start | bytes 98312 | tf_op jit(solution)/shard_map/ppermute | solution.py:282
  19.2 0.5 %collective-permute-start.2 = (bf16[128,128]{1,0:T(8,128)(2,1)S(1)}, bf16[128,128]{1,0:T(8,128)(2,1)S(1)}, u32[]{:S(2)}, u32[]{:S(2)}) collective-permute-start(bf16[128,128]{1,0:T(8,128)(2,1)S(1)} %get-tuple-element.23), channel_id=1, source_target_pairs={{1,2},{2,1},{3,4},{4,3},{5,6},{6,5},{7,8},{8,7},{9,10},{10,9},{11,... | collective-permute-start | bytes 98312 | tf_op jit(solution)/shard_map/ppermute | solution.py:281
  19.8 0.0 collective-permute-done.5.across_ref
  19.8 0.0 collective-permute-done.4.ahead_ref
  19.8 0.0 collective-permute-done.3.behind_ref
  19.8 0.2 shard_map.90
  20.0 1.7 %collective-permute-start.6 = (bf16[4,64,128]{2,1,0:T(8,128)(2,1)S(1)}, bf16[4,64,128]{2,1,0:T(8,128)(2,1)S(1)}, u32[]{:S(2)}, u32[]{:S(2)}) collective-permute-start(bf16[4,64,128]{2,1,0:T(8,128)(2,1)S(1)} %get-tuple-element.29), channel_id=1, source_target_pairs={{0,128},{16,144},{32,160},{48,176},{64,192},{80,208},{96,224},{112... | collective-permute-start | bytes 196616 | tf_op jit(solution)/shard_map/ppermute | solution.py:286
  21.7 0.0 collective-permute-done.1.first_ref
  21.7 5.5 %collective-permute-done.2.second_ref = bf16[128,128]{1,0:T(8,128)(2,1)S(1)} collective-permute-done((bf16[128,128]{1,0:T(8,128)(2,1)S(1)}, bf16[128,128]{1,0:T(8,128)(2,1)S(1)}, u32[]{:S(2)}, u32[]{:S(2)}) %collective-permute-start.2) | collective-permute-done | bytes 32800 | tf_op jit(solution)/shard_map/ppermute | solution.py:281
  27.1 3.7 %shard_map.91 = (f32[4,64,128]{2,1,0:T(8,128)S(1)}, f32[4,64,128]{2,1,0:T(8,128)S(1)}) custom-call(bf16[1,5,64,64,128]{4,3,2,1,0:T(8,128)(2,1)S(1)} %copy-done.2, bf16[1,4,64,128]{3,2,1,0:T(8,128)(2,1)S(1)} %copy-done.1, bf16[256,512]{1,0:T(8,128)(2,1)S(1)} %get-tuple-element.16.near_matrix_ref, bf16[512,256]{1,0:T(8,128)(2,1)S(1)} %get-tuple-element.17.send_matrix_ref, ...), custom_call_target="tpu_custom_call" | custom-call | flops 4294967296 | bytes 6291456 | tf_op jit(solution)/shard_map/pallas_call | solution.py:249
  30.8 0.0 collective-permute-done.6.partner_ref
  30.8 0.7 %shard_map.92 = (bf16[1,4,64,128]{3,2,1,0:T(8,128)(2,1)}, bf16[1,4,64,128]{3,2,1,0:T(8,128)(2,1)}) custom-call(f32[4,64,128]{2,1,0:T(8,128)S(1)} %get-tuple-element.27.image_ref, f32[4,64,128]{2,1,0:T(8,128)S(1)} %get-tuple-element.28.sum_ref, f32[4,64,128]{2,1,0:T(8,128)S(1)} %get-tuple-element.26.after_ref.keep_ref, ...), custom_call_target="tpu_custom_call" | custom-call | bytes 524288 | tf_op jit(solution)/shard_map/pallas_call | solution.py:249
  (3 shorter events, 0.0 us)
Async XLA Ops:
  0.6 0.8 %copy-start = (bf16[1,4,64,128]{3,2,1,0:T(8,128)(2,1)S(1)}, bf16[1,4,64,128]{3,2,1,0:T(8,128)(2,1)}, u32[]{:S(2)}) copy-start(bf16[1,4,64,128]{3,2,1,0:T(8,128)(2,1)} %adjoint_ref.5) | copy-start | bytes 196612
  0.6 0.9 %copy-start.1 = (bf16[1,4,64,128]{3,2,1,0:T(8,128)(2,1)S(1)}, bf16[1,4,64,128]{3,2,1,0:T(8,128)(2,1)}, u32[]{:S(2)}) copy-start(bf16[1,4,64,128]{3,2,1,0:T(8,128)(2,1)} %tangent_ref.5) | copy-start | bytes 196612
  0.7 2.5 %copy-start.2 = (bf16[1,5,64,64,128]{4,3,2,1,0:T(8,128)(2,1)S(1)}, bf16[1,5,64,64,128]{4,3,2,1,0:T(8,128)(2,1)}, u32[]{:S(2)}) copy-start(bf16[1,5,64,64,128]{4,3,2,1,0:T(8,128)(2,1)} %jac_ref.5) | copy-start | bytes 15728644
  0.7 2.5 %copy-start.5 = (s32[2,32]{1,0:T(2,128)S(1)}, s32[2,32]{1,0:T(2,128)}, u32[]{:S(2)}) copy-start(s32[2,32]{1,0:T(2,128)} %send_high_ref.1) | copy-start | bytes 772
  0.7 2.5 %copy-start.4 = (s32[2,32]{1,0:T(2,128)S(1)}, s32[2,32]{1,0:T(2,128)}, u32[]{:S(2)}) copy-start(s32[2,32]{1,0:T(2,128)} %send_low_ref.1) | copy-start | bytes 772
  0.7 2.5 %copy-start.3 = (s32[2,4,128]{2,1,0:T(4,128)S(1)}, s32[2,4,128]{2,1,0:T(4,128)}, u32[]{:S(2)}) copy-start(s32[2,4,128]{2,1,0:T(4,128)} %near_ref.1) | copy-start | bytes 12292
  1.5 4.0 %collective-permute-start = (bf16[1,4,64,128]{3,2,1,0:T(8,128)(2,1)S(1)}, bf16[1,4,64,128]{3,2,1,0:T(8,128)(2,1)S(1)}, u32[]{:S(2)}, u32[]{:S(2)}) collective-permute-start(bf16[1,4,64,128]{3,2,1,0:T(8,128)(2,1)S(1)} %broadcast_select_fusion), channel_id=1, source_target_pairs={{0,128},{16,144},{32,160},{48,176},{64,192},{80,208},{96,224},{112... | collective-permute-start | bytes 196616 | tf_op jit(solution)/shard_map/ppermute | solution.py:286
  5.6 14.2 %collective-permute-start.4 = (bf16[2,4,64,128]{3,2,1,0:T(8,128)(2,1)S(1)}, bf16[2,4,64,128]{3,2,1,0:T(8,128)(2,1)S(1)}, u32[]{:S(2)}, u32[]{:S(2)}) collective-permute-start(bf16[2,4,64,128]{3,2,1,0:T(8,128)(2,1)S(1)} %get-tuple-element.20.after_ref.pair_ref), channel_id=1, source_target_pairs={{0,96},{16,112},{32,0},{48,16},{64,32},{80,48},{96,64},{112,80},{1... | collective-permute-start | bytes 393224 | tf_op jit(solution)/shard_map/ppermute | solution.py:286
  11.7 8.1 %collective-permute-start.3 = (bf16[2,4,64,128]{3,2,1,0:T(8,128)(2,1)S(1)}, bf16[2,4,64,128]{3,2,1,0:T(8,128)(2,1)S(1)}, u32[]{:S(2)}, u32[]{:S(2)}) collective-permute-start(bf16[2,4,64,128]{3,2,1,0:T(8,128)(2,1)S(1)} %get-tuple-element.20.after_ref.pair_ref), channel_id=1, source_target_pairs={{0,32},{16,48},{32,64},{48,80},{64,96},{80,112},{96,0},{112,16},{1... | collective-permute-start | bytes 393224 | tf_op jit(solution)/shard_map/ppermute | solution.py:286
  11.7 8.1 %collective-permute-start.5 = (bf16[4,64,128]{2,1,0:T(8,128)(2,1)S(1)}, bf16[4,64,128]{2,1,0:T(8,128)(2,1)S(1)}, u32[]{:S(2)}, u32[]{:S(2)}) collective-permute-start(bf16[4,64,128]{2,1,0:T(8,128)(2,1)S(1)} %get-tuple-element.21.after_too_ref), channel_id=1, source_target_pairs={{0,64},{16,80},{32,96},{48,112},{64,0},{80,16},{96,32},{112,48},{1... | collective-permute-start | bytes 196616 | tf_op jit(solution)/shard_map/ppermute | solution.py:286
  17.3 4.4 %collective-permute-start.1 = (bf16[128,128]{1,0:T(8,128)(2,1)S(1)}, bf16[128,128]{1,0:T(8,128)(2,1)S(1)}, u32[]{:S(2)}, u32[]{:S(2)}) collective-permute-start(bf16[128,128]{1,0:T(8,128)(2,1)S(1)} %get-tuple-element.22), channel_id=1, source_target_pairs={{0,1},{1,0},{2,3},{3,2},{4,5},{5,4},{6,7},{7,6},{8,9},{9,8},{10,11... | collective-permute-start | bytes 98312 | tf_op jit(solution)/shard_map/ppermute | solution.py:282
  19.2 7.9 %collective-permute-start.2 = (bf16[128,128]{1,0:T(8,128)(2,1)S(1)}, bf16[128,128]{1,0:T(8,128)(2,1)S(1)}, u32[]{:S(2)}, u32[]{:S(2)}) collective-permute-start(bf16[128,128]{1,0:T(8,128)(2,1)S(1)} %get-tuple-element.23), channel_id=1, source_target_pairs={{1,2},{2,1},{3,4},{4,3},{5,6},{6,5},{7,8},{8,7},{9,10},{10,9},{11,... | collective-permute-start | bytes 98312 | tf_op jit(solution)/shard_map/ppermute | solution.py:281
  20.0 10.8 %collective-permute-start.6 = (bf16[4,64,128]{2,1,0:T(8,128)(2,1)S(1)}, bf16[4,64,128]{2,1,0:T(8,128)(2,1)S(1)}, u32[]{:S(2)}, u32[]{:S(2)}) collective-permute-start(bf16[4,64,128]{2,1,0:T(8,128)(2,1)S(1)} %get-tuple-element.29), channel_id=1, source_target_pairs={{0,128},{16,144},{32,160},{48,176},{64,192},{80,208},{96,224},{112... | collective-permute-start | bytes 196616 | tf_op jit(solution)/shard_map/ppermute | solution.py:286
